TPU v7x, 128 devices: a whole 4x4x4 slice. The times are simulated.
128 devices in a mesh: ty: 16 (over y, x), tx: 8 (over z, core).
Axes of the slice: x: 4, y: 4, z: 4, core: 2. Of those that a mesh axis runs over, the one named last changes fastest.
Arguments:
- object_field: float32 [2, 8192, 4096], P(None, 'ty', 'tx'), may hold values from -4 to 4
- probe: float32 [2, 256, 256], replicated, may hold values from -5 to 5
- moduli: float32 [1536, 256, 256], P(('ty', 'tx')), may hold values from 0.2 to 2
- positions: int32 [1536, 2], P(('ty', 'tx')), may hold values from 0 to 7936, as said below
- counts: int32 [128], replicated, may hold values from 1 to 12, as said below
Outputs:
- object_out: float32 [2, 8192, 4096], P(None, 'ty', 'tx')
- probe_out: float32 [2, 256, 256], replicated
Inputs may be any that keep to these rules, and one draw needn't show every extreme that they name: `positions`: slots i * 12 to (i + 1) * 12 - 1 belong to device i (tile-row-major over the 16 x 4096 / 512 tiles); each holds the corner of a patch that starts inside that device's tile and lies wholly inside the object. `counts`: entry i is the number of leading slots of device i that are in use; some entry equals 12.
All inputs are finite; a program needn't handle non-finite values.
Results may differ from a plain program's by a relative error of at most 0.0001.
Values sent between devices are 32-bit elements; how exact they have to be, the bound alone decides.
A program may use at most 128 MiB of HBM per device.

v0:
```python
import math

import jax
import jax.numpy as jnp
from jax import lax
from jax.sharding import PartitionSpec as P

ITERS = 2


step_object = 1.0
tiny_value = 1e-06
floor_sq = 0.0625


def shifted(block, axis, distance):
    devices = range(lax.axis_size(axis))
    route = [(i - distance, i) for i in devices if i - distance in devices]
    return lax.ppermute(block, axis, route)


def tables(length):
    row_ids = lax.broadcasted_iota(jnp.int32, (length, length), 0)
    col_ids = lax.broadcasted_iota(jnp.int32, (length, length), 1)
    angles = (row_ids * col_ids % length).astype(jnp.float32) * (2.0 * math.pi / length)
    factor = 1.0 / math.sqrt(length)
    return (jnp.cos(angles) * factor, jnp.sin(angles) * factor)


def product(left_matrix, right_matrix):
    return jnp.dot(
        left_matrix,
        right_matrix,
        precision=lax.Precision.HIGHEST,
        preferred_element_type=jnp.float32,
    )


def transform(field_real, field_imag, cosine_table, sine_signed):
    left_real = product(cosine_table, field_real) - product(sine_signed, field_imag)
    left_imag = product(cosine_table, field_imag) + product(sine_signed, field_real)
    out_real = product(left_real, cosine_table) - product(left_imag, sine_signed)
    out_imag = product(left_imag, cosine_table) + product(left_real, sine_signed)
    return (out_real, out_imag)


def correct(patch_block, probe_now, modulus, cosine_table, sine_table, weight):
    probe_real = probe_now[0]
    probe_imag = probe_now[1]
    patch_real = patch_block[0]
    patch_imag = patch_block[1]
    exit_real = probe_real * patch_real - probe_imag * patch_imag
    exit_imag = probe_real * patch_imag + probe_imag * patch_real
    wave_real, wave_imag = transform(exit_real, exit_imag, cosine_table, -sine_table)
    scaling = modulus / jnp.sqrt(wave_real * wave_real + wave_imag * wave_imag + floor_sq) - 1.0
    delta_real, delta_imag = transform(
        wave_real * scaling, wave_imag * scaling, cosine_table, sine_table
    )
    update = (
        jnp.stack(
            [
                probe_real * delta_real + probe_imag * delta_imag,
                probe_real * delta_imag - probe_imag * delta_real,
            ]
        )
        * weight
    )
    numer_term = jnp.stack(
        [
            patch_real * delta_real + patch_imag * delta_imag,
            patch_real * delta_imag - patch_imag * delta_real,
        ]
    )
    denom_term = patch_real * patch_real + patch_imag * patch_imag
    return (update, numer_term, denom_term)


def extend(object_now, rim_width):
    lower_rows = shifted(object_now[:, :rim_width, :], "ty", -1)
    tall_block = jnp.concatenate([object_now, lower_rows], 1)
    right_cols = shifted(tall_block[:, :, :rim_width], "tx", -1)
    return jnp.concatenate([tall_block, right_cols], 2)


def fold(object_sums, rim_width, tile_rows, tile_cols):
    right_part = shifted(object_sums[:, :, tile_cols:], "tx", 1)
    object_sums = object_sums.at[:, :, :rim_width].add(right_part)
    lower_part = shifted(object_sums[:, tile_rows:, :tile_cols], "ty", 1)
    return object_sums[:, :tile_rows, :tile_cols].at[:, :rim_width, :].add(lower_part)


def shards(object_field, probe, moduli, positions, counts):
    rim_width = probe.shape[1]
    tile_rows = object_field.shape[1]
    tile_cols = object_field.shape[2]
    grid_cols = lax.axis_size("tx")
    row_index = lax.axis_index("ty")
    col_index = lax.axis_index("tx")
    anchor = jnp.stack([row_index * tile_rows, col_index * tile_cols])
    offsets = positions - anchor[None, :]
    own_count = counts[row_index * grid_cols + col_index]
    cosine_table, sine_table = tables(rim_width)
    zero_index = jnp.int32(0)
    object_now = object_field
    probe_now = probe
    extended = extend(object_now, rim_width)
    for iteration in range(ITERS):
        probe_peak = jnp.max(probe_now[0] * probe_now[0] + probe_now[1] * probe_now[1])
        weight = step_object / (probe_peak + tiny_value)
        current_block = extended

        def visit_slot(slot_id, totals):
            object_sums, probe_numer, probe_denom = totals
            corner_at = (zero_index, offsets[slot_id, 0], offsets[slot_id, 1])
            patch_block = lax.dynamic_slice(current_block, corner_at, (2, rim_width, rim_width))
            update, numer_term, denom_term = correct(
                patch_block, probe_now, moduli[slot_id], cosine_table, sine_table, weight
            )
            current = lax.dynamic_slice(object_sums, corner_at, (2, rim_width, rim_width))
            object_sums = lax.dynamic_update_slice(object_sums, current + update, corner_at)
            return (object_sums, probe_numer + numer_term, probe_denom + denom_term)

        start_totals = (
            jnp.zeros_like(current_block),
            jnp.zeros_like(probe_now),
            jnp.zeros(probe_now.shape[1:], jnp.float32),
        )
        object_sums, probe_numer, probe_denom = lax.fori_loop(
            0, own_count, visit_slot, start_totals
        )
        probe_numer, probe_denom = lax.psum((probe_numer, probe_denom), ("ty", "tx"))
        object_now = object_now + fold(object_sums, rim_width, tile_rows, tile_cols)
        if iteration + 1 < ITERS:
            extended = extend(object_now, rim_width)
        probe_now = probe_now + probe_numer / (probe_denom[None] + tiny_value)
    return (object_now, probe_now)


def solution(mesh):
    return jax.shard_map(
        shards,
        mesh=mesh,
        in_specs=(
            P(None, "ty", "tx"),
            P(),
            P(("ty", "tx"), None, None),
            P(("ty", "tx"), None),
            P(),
        ),
        out_specs=(P(None, "ty", "tx"), P()),
        check_vma=False,
    )
```

profile of v0, /device:TPU:1, one launch (start us, length us, event | category | flops | bytes accessed | tf_op | source)
XLA Modules:
  0.0 1489.3 jit_solution(6285871222105744243)
XLA Ops:
  10.2 24.8 %collective-permute-done = f32[2,256,512]{2,1,0:T(8,128)S(1)} collective-permute-done((f32[2,256,512]{2,1,0:T(8,128)S(1)}, f32[2,256,512]{2,1,0:T(8,128)S(1)}, u32[]{:S(2)}, u32[]{:S(2)}) %collective-permute-start) | collective-permute-done | bytes 1048608 | tf_op jit(solution)/shard_map/ppermute | solution.py:19
  35.1 1.6 copy-done.2
  38.0 3.6 collective-permute-start.1
  44.0 17.7 %collective-permute-done.1 = f32[2,768,256]{2,1,0:T(8,128)S(1)} collective-permute-done((f32[2,768,256]{2,1,0:T(8,128)}, f32[2,768,256]{2,1,0:T(8,128)S(1)}, u32[]{:S(2)}, u32[]{:S(2)}) %collective-permute-start.1) | collective-permute-done | bytes 1572896 | tf_op jit(solution)/shard_map/ppermute | solution.py:19
  61.7 4.4 pad_maximum_fusion
  66.2 2.5 broadcast.122.clone
  68.7 123.2 %while.40 = (s32[]{:T(128)}, f32[2,768,768]{2,1,0:T(8,128)}, f32[2,256,256]{2,1,0:T(8,128)S(1)}, f32[256,256]{1,0:T(8,128)S(1)}, s32[]{:T(128)}, /*index=5*/s32[...) while((s32[]{:T(128)}, f32[2,768,768]{2,1,0:T(8,128)}, ...), condition=%wide.region_2.3_spmd.clone.clone, body=%wide.region_1.2_spmd.clone.clone.sunk | while | flops 3240361984 | bytes 19661128 | solution.py:128
  85.6 2.5 fusion.348
  98.4 2.8 add_bitcast_fusion.4
  101.2 1.5 fusion.353
  102.7 6.8 dynamic_update_slice.18
  126.3 2.5 fusion.348
  139.1 2.8 add_bitcast_fusion.4
  141.9 1.5 fusion.353
  143.4 6.8 dynamic_update_slice.18
  167.1 2.5 fusion.348
  179.9 2.8 add_bitcast_fusion.4
  182.7 1.5 fusion.353
  184.2 6.7 dynamic_update_slice.18
  192.0 1.8 slice.197
  193.8 163.3 %collective-permute-start.2 = (f32[2,768,256]{2,1,0:T(8,128)S(1)}, f32[2,768,256]{2,1,0:T(8,128)S(1)}, u32[]{:S(2)}, u32[]{:S(2)}) collective-permute-start(f32[2,768,256]{2,1,0:T(8,128)S(1)} %slice.197), channel_id=1, source_target_pairs={{0,1},{1,2},{2,3},{3,4},{4,5},{5,6},{6,7},{8,9},{9,10},{10,11},{11... | collective-permute-start | bytes 4718600 | tf_op jit(solution)/shard_map/ppermute | solution.py:19
  357.1 188.6 %collective-permute-done.2 = f32[2,768,256]{2,1,0:T(8,128)S(1)} collective-permute-done((f32[2,768,256]{2,1,0:T(8,128)S(1)}, f32[2,768,256]{2,1,0:T(8,128)S(1)}, u32[]{:S(2)}, u32[]{:S(2)}) %collective-permute-start.2) | collective-permute-done | bytes 1572896 | tf_op jit(solution)/shard_map/ppermute | solution.py:19
  545.7 2.9 add_dynamic-update-slice_fusion.1
  549.9 1.5 collective-permute-start.3
  551.4 1.8 slice.227
  553.2 20.8 %collective-permute-done.3 = f32[2,256,512]{2,1,0:T(8,128)S(1)} collective-permute-done((f32[2,256,512]{2,1,0:T(8,128)S(1)}, f32[2,256,512]{2,1,0:T(8,128)S(1)}, u32[]{:S(2)}, u32[]{:S(2)}) %collective-permute-start.3) | collective-permute-done | bytes 1048608 | tf_op jit(solution)/shard_map/ppermute | solution.py:19
  577.3 25.6 %collective-permute-done.4 = f32[2,256,512]{2,1,0:T(8,128)S(1)} collective-permute-done((f32[2,256,512]{2,1,0:T(8,128)S(1)}, f32[2,256,512]{2,1,0:T(8,128)S(1)}, u32[]{:S(2)}, u32[]{:S(2)}) %collective-permute-start.4) | collective-permute-done | bytes 1048608 | tf_op jit(solution)/shard_map/ppermute | solution.py:19
  605.3 3.2 collective-permute-start.5
  608.5 182.6 %all-reduce.7.cloned.1.call-done = (f32[2,256,256]{2,1,0:T(8,128)}, f32[256,256]{1,0:T(8,128)}) async-done(((f32[2,256,256]{2,1,0:T(8,128)}, f32[256,256]{1,0:T(8,128)}), (f32[2,256,256]{2,1,0:T(8,128)}, f32[256,256]{1,0:T(8,128)})) %all-reduce.7.cloned.1.call-update) | async-done | bytes 786448 | tf_op jit(solution)/shard_map/psum | solution.py:131
  794.6 4.2 pad_maximum_fusion.1
  799.6 2.5 broadcast.122
  802.1 124.9 %while.41 = (s32[]{:T(128)}, f32[2,768,768]{2,1,0:T(8,128)}, f32[2,256,256]{2,1,0:T(8,128)}, f32[256,256]{1,0:T(8,128)S(1)}, s32[]{:T(128)}, /*index=5*/s32[12,2...) while((s32[]{:T(128)}, f32[2,768,768]{2,1,0:T(8,128)}, ...), condition=%wide.region_7.8_spmd.clone.clone, body=%wide.region_6.7_spmd.clone.clone.sunk | while | flops 3240361984 | bytes 19661128 | solution.py:128
  813.0 1.5 convolution_add_fusion.17
  818.9 2.5 fusion.378
  822.8 1.5 convolution_add_fusion.18
  830.2 1.5 convolution_add_fusion.19
  831.7 2.8 add_bitcast_fusion.5
  834.5 2.3 fusion.383
  836.8 6.8 dynamic_update_slice.19
  854.3 1.5 convolution_add_fusion.17
  860.2 2.5 fusion.378
  864.1 1.5 convolution_add_fusion.18
  871.5 1.5 convolution_add_fusion.19
  873.0 2.8 add_bitcast_fusion.5
  875.8 2.3 fusion.383
  878.2 6.8 dynamic_update_slice.19
  895.6 1.5 convolution_add_fusion.17
  901.5 2.5 fusion.378
  905.4 1.5 convolution_add_fusion.18
  912.8 1.5 convolution_add_fusion.19
  914.3 2.8 add_bitcast_fusion.5
  917.1 2.3 fusion.383
  919.4 6.7 dynamic_update_slice.19
  927.0 1.6 slice.206
  928.7 166.9 %collective-permute-start.6 = (f32[2,768,256]{2,1,0:T(8,128)S(1)}, f32[2,768,256]{2,1,0:T(8,128)S(1)}, u32[]{:S(2)}, u32[]{:S(2)}) collective-permute-start(f32[2,768,256]{2,1,0:T(8,128)S(1)} %slice.206), channel_id=1, source_target_pairs={{0,1},{1,2},{2,3},{3,4},{4,5},{5,6},{6,7},{8,9},{9,10},{10,11},{11... | collective-permute-start | bytes 4718600 | tf_op jit(solution)/shard_map/ppermute | solution.py:19
  1095.5 207.5 %collective-permute-done.6 = f32[2,768,256]{2,1,0:T(8,128)S(1)} collective-permute-done((f32[2,768,256]{2,1,0:T(8,128)S(1)}, f32[2,768,256]{2,1,0:T(8,128)S(1)}, u32[]{:S(2)}, u32[]{:S(2)}) %collective-permute-start.6) | collective-permute-done | bytes 1572896 | tf_op jit(solution)/shard_map/ppermute | solution.py:19
  1303.1 2.9 add_dynamic-update-slice_fusion
  1305.9 2.3 slice.235
  1308.2 2.3 collective-permute-start.7
  1310.5 163.4 %all-reduce.5.cloned.1.call-done = (f32[2,256,256]{2,1,0:T(8,128)}, f32[256,256]{1,0:T(8,128)}) async-done(((f32[2,256,256]{2,1,0:T(8,128)}, f32[256,256]{1,0:T(8,128)}), (f32[2,256,256]{2,1,0:T(8,128)}, f32[256,256]{1,0:T(8,128)})) %all-reduce.5.cloned.1.call-update) | async-done | bytes 786448 | tf_op jit(solution)/shard_map/psum | solution.py:131
  1474.9 1.9 divide_add_fusion
  1476.9 1.8 slice.233
  1478.7 1.8 fusion.228
  1480.4 1.8 add.386
  (135 shorter events, 139.3 us)
Async XLA Ops:
  7.2 2.8 copy-start.3
  7.2 783.9 %all-reduce.7.cloned.1.call-start = ((), (), s32[]{:S(2)}) async-start(), calls=%async_computation.1 | async-start | bytes 1572864 | tf_op jit(solution)/shard_map/psum | solution.py:131
  8.7 26.3 %collective-permute-start = (f32[2,256,512]{2,1,0:T(8,128)S(1)}, f32[2,256,512]{2,1,0:T(8,128)S(1)}, u32[]{:S(2)}, u32[]{:S(2)}) collective-permute-start(f32[2,256,512]{2,1,0:T(8,128)S(1)} %slice.192), channel_id=1, source_target_pairs={{8,0},{16,8},{24,16},{32,24},{40,32},{48,40},{56,48},{64,56},{72,6... | collective-permute-start | bytes 3145736 | tf_op jit(solution)/shard_map/ppermute | solution.py:19
  10.2 31.5 %copy-start = (f32[2,256,256]{2,1,0:T(8,128)S(1)}, f32[2,256,256]{2,1,0:T(8,128)}, u32[]{:S(2)}) copy-start(f32[2,256,256]{2,1,0:T(8,128)} %param.18) | copy-start | bytes 1572868
  10.2 33.0 %copy-start.9 = (s32[128]{0:T(128)S(1)}, s32[128]{0:T(128)}, u32[]{:S(2)}) copy-start(s32[128]{0:T(128)} %param.21) | copy-start | bytes 1540
  10.2 33.7 %copy-start.8 = (s32[12,2]{0,1:T(2,128)S(1)}, s32[12,2]{0,1:T(2,128)}, u32[]{:S(2)}) copy-start(s32[12,2]{0,1:T(2,128)} %param.20) | copy-start | bytes 292
  35.1 1.7 copy-start.2
  38.0 23.7 %collective-permute-start.1 = (f32[2,768,256]{2,1,0:T(8,128)}, f32[2,768,256]{2,1,0:T(8,128)S(1)}, u32[]{:S(2)}, u32[]{:S(2)}) collective-permute-start(f32[2,768,256]{2,1,0:T(8,128)} %slice.226), channel_id=1, source_target_pairs={{1,0},{2,1},{3,2},{4,3},{5,4},{6,5},{7,6},{9,8},{10,9},{11,10},{12... | collective-permute-start | bytes 4718600 | tf_op jit(solution)/shard_map/ppermute | solution.py:19
  191.9 356.7 %copy-start.1 = (f32[2,256,256]{2,1,0:T(8,128)}, f32[2,256,256]{2,1,0:T(8,128)S(1)}, u32[]{:S(2)}) copy-start(f32[2,256,256]{2,1,0:T(8,128)S(1)} %get-tuple-element.449) | copy-start | bytes 1572868
  191.9 356.7 %copy-start.6 = (f32[256,256]{1,0:T(8,128)}, f32[256,256]{1,0:T(8,128)S(1)}, u32[]{:S(2)}) copy-start(f32[256,256]{1,0:T(8,128)S(1)} %get-tuple-element.450) | copy-start | bytes 786436
  193.8 352.0 %collective-permute-start.2 = (f32[2,768,256]{2,1,0:T(8,128)S(1)}, f32[2,768,256]{2,1,0:T(8,128)S(1)}, u32[]{:S(2)}, u32[]{:S(2)}) collective-permute-start(f32[2,768,256]{2,1,0:T(8,128)S(1)} %slice.197), channel_id=1, source_target_pairs={{0,1},{1,2},{2,3},{3,4},{4,5},{5,6},{6,7},{8,9},{9,10},{10,11},{11... | collective-permute-start | bytes 4718600 | tf_op jit(solution)/shard_map/ppermute | solution.py:19
  549.9 25.5 %copy-start.4 = (f32[2,512,512]{2,1,0:T(8,128)S(1)}, f32[2,512,512]{2,1,0:T(8,128)}, u32[]{:S(2)}) copy-start(f32[2,512,512]{2,1,0:T(8,128)} %param.17) | copy-start | bytes 6291460
  549.9 24.1 %collective-permute-start.3 = (f32[2,256,512]{2,1,0:T(8,128)S(1)}, f32[2,256,512]{2,1,0:T(8,128)S(1)}, u32[]{:S(2)}, u32[]{:S(2)}) collective-permute-start(f32[2,256,512]{2,1,0:T(8,128)S(1)} %slice.229), channel_id=1, source_target_pairs={{0,8},{8,16},{16,24},{24,32},{32,40},{40,48},{48,56},{56,64},{64,7... | collective-permute-start | bytes 3145736 | tf_op jit(solution)/shard_map/ppermute | solution.py:19
  576.0 26.9 %collective-permute-start.4 = (f32[2,256,512]{2,1,0:T(8,128)S(1)}, f32[2,256,512]{2,1,0:T(8,128)S(1)}, u32[]{:S(2)}, u32[]{:S(2)}) collective-permute-start(f32[2,256,512]{2,1,0:T(8,128)S(1)} %slice.230), channel_id=1, source_target_pairs={{8,0},{16,8},{24,16},{32,24},{40,32},{48,40},{56,48},{64,56},{72,6... | collective-permute-start | bytes 3145736 | tf_op jit(solution)/shard_map/ppermute | solution.py:19
  603.0 1.0 copy-start.7
  605.3 189.3 %collective-permute-start.5 = (f32[2,768,256]{2,1,0:T(8,128)}, f32[2,768,256]{2,1,0:T(8,128)}, u32[]{:S(2)}, u32[]{:S(2)}) collective-permute-start(f32[2,768,256]{2,1,0:T(8,128)} %pad_maximum_fusion.2), channel_id=1, source_target_pairs={{1,0},{2,1},{3,2},{4,3},{5,4},{6,5},{7,6},{9,8},{10,9},{11,10},{12... | collective-permute-start | bytes 4718600 | tf_op jit(solution)/shard_map/ppermute | solution.py:19
  608.5 865.5 %all-reduce.5.cloned.1.call-start = ((), (), s32[]{:S(2)}) async-start(), calls=%async_computation | async-start | bytes 1572864 | tf_op jit(solution)/shard_map/psum | solution.py:131
  927.0 378.9 %copy-start.5 = (f32[256,256]{1,0:T(8,128)}, f32[256,256]{1,0:T(8,128)S(1)}, u32[]{:S(2)}) copy-start(f32[256,256]{1,0:T(8,128)S(1)} %get-tuple-element.453) | copy-start | bytes 786436
  928.7 374.4 %collective-permute-start.6 = (f32[2,768,256]{2,1,0:T(8,128)S(1)}, f32[2,768,256]{2,1,0:T(8,128)S(1)}, u32[]{:S(2)}, u32[]{:S(2)}) collective-permute-start(f32[2,768,256]{2,1,0:T(8,128)S(1)} %slice.206), channel_id=1, source_target_pairs={{0,1},{1,2},{2,3},{3,4},{4,5},{5,6},{6,7},{8,9},{9,10},{10,11},{11... | collective-permute-start | bytes 4718600 | tf_op jit(solution)/shard_map/ppermute | solution.py:19
  1308.2 170.4 %collective-permute-start.7 = (f32[2,256,512]{2,1,0:T(8,128)}, f32[2,256,512]{2,1,0:T(8,128)}, u32[]{:S(2)}, u32[]{:S(2)}) collective-permute-start(f32[2,256,512]{2,1,0:T(8,128)} %slice.235), channel_id=1, source_target_pairs={{0,8},{8,16},{16,24},{24,32},{32,40},{40,48},{48,56},{56,64},{64,7... | collective-permute-start | bytes 3145736 | tf_op jit(solution)/shard_map/ppermute | solution.py:19
Sparse Core Ops, SparseCore 0:
  608.6 182.4 all-reduce.6
  1310.7 163.2 all-reduce.4
where the time goes:
time: 1500 us; the launch traced here: 1490 us
  waiting for transfers between devices  831 us (55%)
  starting transfers between devices  343 us (23%)
  matrix products  155 us (10%)
  local copies, waits for them, and re-layouts  67 us (4%)
  other arithmetic  47.3 us (3%)
  loops' own time  29.4 us (2%)
  between operations  16 us (1%)
    ppermute x8, waiting for transfers between devices, shifted(): return lax.ppermute(block, axis, route)  485 us
    psum x2, waiting for transfers between devices, shards(): lax.psum((probe_numer, probe_denom), ('ty', 'tx'))  346 us
    ppermute x8, starting transfers between devices, shifted(): return lax.ppermute(block, axis, route)  343 us
    dot_general x96, matrix products, product(): jnp.dot(left_matrix, right_matrix, precision=lax.Precision.HIGHEST, prefe...  155 us
    dynamic_update_slice x6, local copies, waits for them, and re-layouts, visit_slot(): lax.dynamic_update_slice(object_sums, current + update, corner_at)  40.5 us
  transfers between devices with their start and end apart: 10, of which 8 were waited for; matrix products, arithmetic and copies ran while one was open for 1% of the time, Pallas kernels for 0%

commit v1 on v0

v1 whole, which is shorter than its diff:
```python
import math

import jax
import jax.numpy as jnp
import ml_dtypes
import numpy as np
from jax import lax
from jax.experimental import pallas as pl
from jax.experimental.pallas import tpu as pltpu
from jax.sharding import PartitionSpec as P

F32 = jnp.float32
BF16 = jnp.bfloat16
MESH = pl.DeviceIdType.MESH

PATCH = 256
HALF = 128
TILE = 512
EXT = 768
CAP = 12
CHUNKS = 4
CHUNK = PATCH // CHUNKS
tiny_value = 1e-06
floor_sq = 0.0625

Z0 = slice(0, 256)
Z1 = slice(256, 512)
Z2 = slice(512, 768)


def dft_tables():
    rows = np.arange(HALF)[:, None]
    cols = np.arange(HALF)[None, :]
    parts = []
    for odd in (0, 1):
        wave = np.exp(-2j * math.pi * ((rows * (2 * cols + odd)) % PATCH) / PATCH) / 16.0
        table = np.block([[wave.real, wave.imag], [-wave.imag, wave.real]])
        for form in (table, table.T):
            high = form.astype(np.float32).astype(ml_dtypes.bfloat16)
            low = (form - high.astype(np.float64)).astype(ml_dtypes.bfloat16)
            parts += [high, low]
    return np.stack(parts)


def order_table():
    table = np.zeros((PATCH, PATCH), np.float32)
    for col in range(PATCH):
        table[2 * (col % HALF) + col // HALF, col] = 1.0
    return np.stack([table.T, table]).astype(ml_dtypes.bfloat16)


def dot(left, right):
    return jnp.dot(left, right, preferred_element_type=F32)


def split(value):
    high = value.astype(BF16)
    return high, (value - high.astype(F32)).astype(BF16)


def thirds(value):
    high = value.astype(BF16)
    rest = value - high.astype(F32)
    middle = rest.astype(BF16)
    return high, middle, (rest - middle.astype(F32)).astype(BF16)


def right_product(value, table, at):
    high, low = split(value)
    return dot(
        jnp.concatenate([high, low, high], 1),
        jnp.concatenate([table[at], table[at], table[at + 1]], 0),
    )


def left_product(table, at, value):
    high, low = split(value)
    return dot(
        jnp.concatenate([table[at], table[at + 1], table[at]], 1),
        jnp.concatenate([high, high, low], 0),
    )


def gather(ref, plane, row, col):
    sub_shift = row % 8
    lane_shift = col % 128
    row_at = pl.multiple_of(row - sub_shift, 8)
    col_at = pl.multiple_of(col - lane_shift, 128)
    lane = lax.broadcasted_iota(jnp.int32, (32, 8, 128), 2)
    sub = lax.broadcasted_iota(jnp.int32, (32, 8, 128), 1)
    cols = []
    for k in range(3):
        block = ref[plane, pl.ds(row_at, 264), pl.ds(col_at + 128 * k, 128)].reshape(33, 8, 128)
        block = pltpu.roll(block, (8 - sub_shift) % 8, 1)
        block = jnp.where(sub < 8 - sub_shift, block[:32], block[1:])
        cols.append(pltpu.roll(block, (128 - lane_shift) % 128, 2))
    parts = [
        jnp.where(lane < 128 - lane_shift, cols[k], cols[k + 1]).reshape(PATCH, 128)
        for k in range(2)
    ]
    return jnp.concatenate(parts, 1)


def scatter_add(ref, plane, row, col, update):
    sub_shift = row % 8
    lane_shift = col % 128
    row_at = pl.multiple_of(row - sub_shift, 8)
    col_at = pl.multiple_of(col - lane_shift, 128)
    lane = lax.broadcasted_iota(jnp.int32, (32, 8, 128), 2)
    sub = lax.broadcasted_iota(jnp.int32, (33, 8, 128), 1)
    first, second = [
        pltpu.roll(update[:, 128 * k : 128 * k + 128].reshape(32, 8, 128), lane_shift, 2)
        for k in range(2)
    ]
    zero = jnp.zeros((32, 8, 128), F32)
    row_of_zeros = jnp.zeros((1, 8, 128), F32)
    right = lane >= lane_shift
    cols = [
        jnp.where(right, first, zero),
        jnp.where(right, second, first),
        jnp.where(right, zero, second),
    ]
    for k in range(3):
        block = pltpu.roll(cols[k], sub_shift, 1)
        block = jnp.where(
            sub >= sub_shift,
            jnp.concatenate([block, row_of_zeros], 0),
            jnp.concatenate([row_of_zeros, block], 0),
        )
        ref[plane, pl.ds(row_at, 264), pl.ds(col_at + 128 * k, 128)] += block.reshape(264, 128)


def scaled(wave, modulus):
    real = wave[:HALF]
    imag = wave[HALF:]
    scale = modulus * lax.rsqrt(real * real + imag * imag + floor_sq) - 1.0
    return jnp.concatenate([real * scale, imag * scale], 0)


def visit(slot, offsets, extended, probe, weighted, moduli, table, sums, totals):
    row = offsets[slot, 0]
    col = offsets[slot, 1]
    patch_real = gather(extended, 0, row, col)
    patch_imag = gather(extended, 1, row, col)
    totals[2] += patch_real * patch_real + patch_imag * patch_imag
    exit_real = probe[0] * patch_real - probe[1] * patch_imag
    exit_imag = probe[0] * patch_imag + probe[1] * patch_real
    even = jnp.concatenate(
        [exit_real[:, :HALF] + exit_real[:, HALF:], exit_imag[:, :HALF] + exit_imag[:, HALF:]], 1
    )
    odd = jnp.concatenate(
        [exit_real[:, :HALF] - exit_real[:, HALF:], exit_imag[:, :HALF] - exit_imag[:, HALF:]], 1
    )
    even = right_product(even, table, 0)
    odd = right_product(odd, table, 4)
    real = jnp.concatenate([even[:, :HALF], odd[:, :HALF]], 1)
    imag = jnp.concatenate([even[:, HALF:], odd[:, HALF:]], 1)
    even = jnp.concatenate([real[:HALF] + real[HALF:], imag[:HALF] + imag[HALF:]], 0)
    odd = jnp.concatenate([real[:HALF] - real[HALF:], imag[:HALF] - imag[HALF:]], 0)
    even = scaled(left_product(table, 2, even), moduli[slot, :HALF])
    odd = scaled(left_product(table, 6, odd), moduli[slot, HALF:])
    even = left_product(table, 0, even)
    odd = left_product(table, 4, odd)
    real = jnp.concatenate([even[:HALF] + odd[:HALF], even[:HALF] - odd[:HALF]], 0)
    imag = jnp.concatenate([even[HALF:] + odd[HALF:], even[HALF:] - odd[HALF:]], 0)
    even = right_product(jnp.concatenate([real[:, :HALF], imag[:, :HALF]], 1), table, 2)
    odd = right_product(jnp.concatenate([real[:, HALF:], imag[:, HALF:]], 1), table, 6)
    delta_real = jnp.concatenate(
        [even[:, :HALF] + odd[:, :HALF], even[:, :HALF] - odd[:, :HALF]], 1
    )
    delta_imag = jnp.concatenate(
        [even[:, HALF:] + odd[:, HALF:], even[:, HALF:] - odd[:, HALF:]], 1
    )
    totals[0] += patch_real * delta_real + patch_imag * delta_imag
    totals[1] += patch_real * delta_imag - patch_imag * delta_real
    scatter_add(sums, 0, row, col, weighted[0] * delta_real + weighted[1] * delta_imag)
    scatter_add(sums, 1, row, col, weighted[0] * delta_imag - weighted[1] * delta_real)


def slots_kernel(count, offsets, extended, probe, moduli, table, sums, totals, weighted):
    peak = jnp.max(probe[0] * probe[0] + probe[1] * probe[1])
    weighted[...] = probe[...] * (1.0 / (peak + tiny_value))
    sums[...] = jnp.zeros_like(sums)
    totals[...] = jnp.zeros_like(totals)

    def step(slot, carry):
        visit(slot, offsets, extended, probe, weighted, moduli, table, sums, totals)
        return carry

    lax.fori_loop(0, count[0], step, 0)


VMEM = pl.BlockSpec(memory_space=pltpu.VMEM)
SMEM = pl.BlockSpec(memory_space=pltpu.SMEM)


def run_slots(count, offsets, extended, probe, moduli, table):
    return pl.pallas_call(
        slots_kernel,
        out_shape=(
            jax.ShapeDtypeStruct((2, EXT, EXT), F32),
            jax.ShapeDtypeStruct((3, PATCH, PATCH), F32),
        ),
        in_specs=[SMEM, SMEM, VMEM, VMEM, VMEM, VMEM],
        out_specs=(VMEM, VMEM),
        scratch_shapes=[pltpu.VMEM((2, PATCH, PATCH), F32)],
        compiler_params=pltpu.CompilerParams(vmem_limit_bytes=56 * 2**20),
        cost_estimate=pl.CostEstimate(
            flops=6 * 10**9, bytes_accessed=14 * 10**6, transcendentals=0
        ),
    )(count, offsets, extended, probe, moduli, table)


class Place:
    def __init__(self):
        ty = lax.axis_index("ty")
        tx = lax.axis_index("tx")
        self.ty, self.tx = ty, tx
        self.y, self.x = ty // 4, ty % 4
        self.z, self.core = tx // 2, tx % 2
        self.up = ((ty + 15) % 16, tx)
        self.down = ((ty + 1) % 16, tx)
        self.left = (ty, (tx + 7) % 8)
        self.right = (ty, (tx + 1) % 8)
        self.other = (ty, self.z * 2 + 1 - self.core)

    def along_y(self, step):
        return (((self.y + step) % 4) * 4 + self.x, self.tx)

    def along_x(self, step):
        return (self.y * 4 + (self.x + step) % 4, self.tx)

    def along_z(self, step):
        return (self.ty, ((self.z + step) % 4) * 2 + self.core)


def greet(devices):
    barrier = pltpu.get_barrier_semaphore()
    for device in devices:
        pl.semaphore_signal(barrier, inc=1, device_id=device, device_id_type=MESH)
    pl.semaphore_wait(barrier, len(devices))


class Copies:
    def __init__(self, send, receive):
        self.send, self.receive, self.used = send, receive, 0

    def start(self, source, target, device):
        copy = pltpu.make_async_remote_copy(
            src_ref=source,
            dst_ref=target,
            send_sem=self.send.at[self.used],
            recv_sem=self.receive.at[self.used],
            device_id=device,
            device_id_type=MESH,
        )
        self.used += 1
        copy.start()
        return copy


def rows_of(zone, chunk):
    return slice(zone.start + chunk * CHUNK, zone.start + (chunk + 1) * CHUNK)


def extend_kernel(tile, moduli, order, extended, ordered, send, receive):
    here = Place()
    copies = Copies(send, receive)
    greet([here.up, here.down, here.left, here.right])
    above = []
    for chunk in range(CHUNKS):
        above.append(
            copies.start(
                tile.at[:, rows_of(Z0, chunk), Z0], extended.at[:, rows_of(Z2, chunk), Z0], here.up
            )
        )
    beside = [copies.start(tile.at[:, :, Z0], extended.at[:, 0:TILE, Z2], here.left)]
    beside.append(copies.start(tile.at[:, Z0, Z1], extended.at[:, Z2, Z1], here.up))
    extended[:, 0:TILE, 0:TILE] = tile[...]

    def reorder(slot, carry):
        block = moduli[slot]
        block = sum(dot(order[0], part) for part in thirds(block))
        ordered[slot] = sum(dot(part, order[1]) for part in thirds(block))
        return carry

    lax.fori_loop(0, CAP, reorder, 0)
    for chunk in range(CHUNKS):
        above[chunk].wait_recv()
        beside.append(
            copies.start(
                extended.at[:, rows_of(Z2, chunk), Z0],
                extended.at[:, rows_of(Z2, chunk), Z2],
                here.left,
            )
        )
    for copy in above:
        copy.wait_send()
    for copy in beside:
        copy.wait()


def extend(tile, moduli, order):
    copies = 2 * CHUNKS + 2
    return pl.pallas_call(
        extend_kernel,
        out_shape=(
            jax.ShapeDtypeStruct((2, EXT, EXT), F32),
            jax.ShapeDtypeStruct((CAP, PATCH, PATCH), F32),
        ),
        in_specs=[VMEM] * 3,
        out_specs=(VMEM, VMEM),
        scratch_shapes=[pltpu.SemaphoreType.DMA((copies,)), pltpu.SemaphoreType.DMA((copies,))],
        compiler_params=pltpu.CompilerParams(
            vmem_limit_bytes=48 * 2**20, collective_id=0, has_side_effects=True
        ),
        cost_estimate=pl.CostEstimate(
            flops=10**9, bytes_accessed=14 * 10**6, transcendentals=0
        ),
    )(tile, moduli, order)


class Reduction:
    def __init__(self, here, copies, totals, probe, probe_out, landed, held):
        self.here, self.copies = here, copies
        self.totals, self.probe, self.probe_out = totals, probe, probe_out
        self.land_core, self.land_y, self.land_x, self.land_z = landed
        self.held_core, self.held_y, self.held_x = held
        self.in_flight = []
        self.sent = []

    def launch(self, source, target, device):
        self.in_flight.append(self.copies.start(source, target, device))

    def arrive(self):
        for copy in self.in_flight:
            copy.wait_recv()
        self.sent += self.in_flight
        self.in_flight = []

    def start(self):
        half = pl.ds(pl.multiple_of((1 - self.here.core) * HALF, HALF), HALF)
        self.launch(self.totals.at[:, half, :], self.land_core, self.here.other)

    def after_core(self):
        self.arrive()
        half = pl.ds(pl.multiple_of(self.here.core * HALF, HALF), HALF)
        self.held_core[...] = self.totals[:, half, :] + self.land_core[...]
        for step in range(1, 4):
            part = pl.ds(pl.multiple_of(((self.here.y + step) % 4) * 32, 32), 32)
            self.launch(
                self.held_core.at[:, part, :], self.land_y.at[step - 1], self.here.along_y(step)
            )

    def after_y(self):
        self.arrive()
        part = pl.ds(pl.multiple_of(self.here.y * 32, 32), 32)
        self.held_y[...] = (self.held_core[:, part, :] + self.land_y[0]) + (
            self.land_y[1] + self.land_y[2]
        )
        for step in range(1, 4):
            part = pl.ds(pl.multiple_of(((self.here.x + step) % 4) * 8, 8), 8)
            self.launch(
                self.held_y.at[:, part, :], self.land_x.at[step - 1], self.here.along_x(step)
            )

    def after_x(self):
        self.arrive()
        part = pl.ds(pl.multiple_of(self.here.x * 8, 8), 8)
        self.held_x[...] = (self.held_y[:, part, :] + self.land_x[0]) + (
            self.land_x[1] + self.land_x[2]
        )
        for step in range(1, 4):
            self.launch(self.held_x, self.land_z.at[self.here.z], self.here.along_z(step))
        self.land_z[self.here.z] = self.held_x[...]

    def share(self, rows):
        start = self.here.core * HALF
        if rows < 128:
            start = start + self.here.y * 32
        if rows < 32:
            start = start + self.here.x * 8
        part = pl.ds(pl.multiple_of(start, rows), rows)
        return self.probe_out.at[:, part, :]

    def after_z(self):
        self.arrive()
        total = (self.land_z[0] + self.land_z[1]) + (self.land_z[2] + self.land_z[3])
        start = self.here.core * HALF + self.here.y * 32 + self.here.x * 8
        part = pl.ds(pl.multiple_of(start, 8), 8)
        self.probe_out[:, part, :] = self.probe[:, part, :] + total[0:2] / (
            total[2:3] + tiny_value
        )
        for step in range(1, 4):
            self.launch(self.share(8), self.share(8), self.here.along_x(step))

    def gather_x(self):
        self.arrive()
        for step in range(1, 4):
            self.launch(self.share(32), self.share(32), self.here.along_y(step))

    def gather_y(self):
        self.arrive()
        self.launch(self.share(128), self.share(128), self.here.other)

    def finish(self):
        self.arrive()
        for copy in self.sent:
            copy.wait_send()


REDUCTION_COPIES = 1 + 3 + 3 + 3 + 3 + 3 + 1


def everyone(here):
    devices = [here.up, here.down, here.left, here.right, here.other]
    for step in range(1, 4):
        devices += [here.along_y(step), here.along_x(step), here.along_z(step)]
    return devices


def exchange_kernel(
    sums, extended, totals, probe, out, probe_out,
    from_left, from_up, from_down, from_right, top, bottom,
    land_core, land_y, land_x, land_z, held_core, held_y, held_x,
    send, receive,
):
    here = Place()
    copies = Copies(send, receive)
    reduction = Reduction(
        here, copies, totals, probe, probe_out,
        (land_core, land_y, land_x, land_z), (held_core, held_y, held_x),
    )
    greet(everyone(here))
    rest = []
    reduction.start()
    left_bottom, left_top = [], []
    for chunk in range(CHUNKS):
        for zone, kept in ((Z2, left_bottom), (Z0, left_top)):
            rows = rows_of(zone, chunk)
            kept.append(copies.start(sums.at[:, rows, Z2], from_left.at[:, rows, :], here.right))
    middle_down = copies.start(sums.at[:, Z2, Z1], from_up.at[:, :, Z1], here.down)
    middle_up = copies.start(sums.at[:, Z0, Z1], from_down.at[:, :, Z1], here.up)
    side_left = copies.start(sums.at[:, Z1, Z0], from_right, here.left)
    side_right = copies.start(sums.at[:, Z1, Z2], from_left.at[:, Z1, :], here.right)
    reduction.after_core()
    out[:, Z1, Z1] = extended[:, Z1, Z1] + sums[:, Z1, Z1]
    reduction.after_y()
    outer = []
    for chunk in range(CHUNKS):
        rows = rows_of(Z0, chunk)
        low = rows_of(Z2, chunk)
        left_bottom[chunk].wait_recv()
        bottom[:, rows, :] = sums[:, low, Z0] + from_left[:, low, :]
        down = copies.start(bottom.at[:, rows, :], from_up.at[:, rows, Z0], here.down)
        left_top[chunk].wait_recv()
        top[:, rows, :] = sums[:, rows, Z0] + from_left[:, rows, :]
        up = copies.start(top.at[:, rows, :], from_down.at[:, rows, Z0], here.up)
        outer.append((down, up))
    reduction.after_x()
    side_left.wait_recv()
    out[:, Z1, Z2] = extended[:, Z1, Z2] + (sums[:, Z1, Z2] + from_right[...])
    middle_down.wait_recv()
    out[:, Z0, Z1] = extended[:, Z0, Z1] + (sums[:, Z0, Z1] + from_up[:, :, Z1])
    middle_up.wait_recv()
    out[:, Z2, Z1] = extended[:, Z2, Z1] + (sums[:, Z2, Z1] + from_down[:, :, Z1])
    reduction.after_z()
    side_right.wait_recv()
    out[:, Z1, Z0] = extended[:, Z1, Z0] + (sums[:, Z1, Z0] + from_left[:, Z1, :])
    reduction.gather_x()
    last = []
    for chunk in range(CHUNKS):
        rows = rows_of(Z0, chunk)
        low = rows_of(Z2, chunk)
        down, up = outer[chunk]
        down.wait_recv()
        out[:, rows, Z0] = extended[:, rows, Z0] + (top[:, rows, :] + from_up[:, rows, Z0])
        last.append(copies.start(out.at[:, rows, Z0], out.at[:, rows, Z2], here.left))
        up.wait_recv()
        out[:, low, Z0] = extended[:, low, Z0] + (bottom[:, rows, :] + from_down[:, rows, Z0])
        last.append(copies.start(out.at[:, low, Z0], out.at[:, low, Z2], here.left))
        if chunk == 1:
            reduction.gather_y()
    reduction.finish()
    for copy in left_bottom + left_top + [middle_down, middle_up, side_left, side_right]:
        copy.wait_send()
    for down, up in outer:
        down.wait_send()
        up.wait_send()
    for copy in last:
        copy.wait()


def reduction_scratch():
    return [
        pltpu.VMEM((3, 128, PATCH), F32),
        pltpu.VMEM((3, 3, 32, PATCH), F32),
        pltpu.VMEM((3, 3, 8, PATCH), F32),
        pltpu.VMEM((4, 3, 8, PATCH), F32),
        pltpu.VMEM((3, 128, PATCH), F32),
        pltpu.VMEM((3, 32, PATCH), F32),
        pltpu.VMEM((3, 8, PATCH), F32),
    ]


def exchange(sums, extended, totals, probe):
    copies = REDUCTION_COPIES + 6 * CHUNKS + 4
    return pl.pallas_call(
        exchange_kernel,
        out_shape=(
            jax.ShapeDtypeStruct((2, EXT, EXT), F32),
            jax.ShapeDtypeStruct((2, PATCH, PATCH), F32),
        ),
        in_specs=[VMEM] * 4,
        out_specs=(VMEM, VMEM),
        scratch_shapes=[
            pltpu.VMEM((2, EXT, PATCH), F32),
            pltpu.VMEM((2, PATCH, TILE), F32),
            pltpu.VMEM((2, PATCH, TILE), F32),
            pltpu.VMEM((2, PATCH, PATCH), F32),
            pltpu.VMEM((2, PATCH, PATCH), F32),
            pltpu.VMEM((2, PATCH, PATCH), F32),
            *reduction_scratch(),
            pltpu.SemaphoreType.DMA((copies,)),
            pltpu.SemaphoreType.DMA((copies,)),
        ],
        compiler_params=pltpu.CompilerParams(
            vmem_limit_bytes=48 * 2**20, collective_id=1, has_side_effects=True
        ),
        cost_estimate=pl.CostEstimate(
            flops=10**9, bytes_accessed=14 * 10**6, transcendentals=0
        ),
    )(sums, extended, totals, probe)


def fold_kernel(
    sums, extended, totals, probe, out, probe_out,
    from_left, from_up, bottom,
    land_core, land_y, land_x, land_z, held_core, held_y, held_x,
    send, receive,
):
    here = Place()
    copies = Copies(send, receive)
    reduction = Reduction(
        here, copies, totals, probe, probe_out,
        (land_core, land_y, land_x, land_z), (held_core, held_y, held_x),
    )
    greet(everyone(here))
    reduction.start()
    corner = []
    for chunk in range(CHUNKS):
        rows = rows_of(Z2, chunk)
        corner.append(copies.start(sums.at[:, rows, Z2], from_left.at[:, rows, :], here.right))
    middle = copies.start(sums.at[:, Z2, Z1], from_up.at[:, :, Z1], here.down)
    side = copies.start(sums.at[:, 0:TILE, Z2], from_left.at[:, 0:TILE, :], here.right)
    reduction.after_core()
    out[:, Z1, Z1] = extended[:, Z1, Z1] + sums[:, Z1, Z1]
    reduction.after_y()
    outer = []
    for chunk in range(CHUNKS):
        rows = rows_of(Z0, chunk)
        low = rows_of(Z2, chunk)
        corner[chunk].wait_recv()
        bottom[:, rows, :] = sums[:, low, Z0] + from_left[:, low, :]
        outer.append(copies.start(bottom.at[:, rows, :], from_up.at[:, rows, Z0], here.down))
    reduction.after_x()
    reduction.after_z()
    side.wait_recv()
    out[:, Z1, Z0] = extended[:, Z1, Z0] + (sums[:, Z1, Z0] + from_left[:, Z1, :])
    reduction.gather_x()
    middle.wait_recv()
    out[:, Z0, Z1] = extended[:, Z0, Z1] + (sums[:, Z0, Z1] + from_up[:, :, Z1])
    reduction.gather_y()
    for chunk in range(CHUNKS):
        rows = rows_of(Z0, chunk)
        outer[chunk].wait_recv()
        out[:, rows, Z0] = extended[:, rows, Z0] + (
            (sums[:, rows, Z0] + from_left[:, rows, :]) + from_up[:, rows, Z0]
        )
    reduction.finish()
    for copy in corner + [middle, side] + outer:
        copy.wait_send()


def fold(sums, extended, totals, probe):
    copies = REDUCTION_COPIES + 2 * CHUNKS + 2
    return pl.pallas_call(
        fold_kernel,
        out_shape=(
            jax.ShapeDtypeStruct((2, TILE, TILE), F32),
            jax.ShapeDtypeStruct((2, PATCH, PATCH), F32),
        ),
        in_specs=[VMEM] * 4,
        out_specs=(VMEM, VMEM),
        scratch_shapes=[
            pltpu.VMEM((2, EXT, PATCH), F32),
            pltpu.VMEM((2, PATCH, TILE), F32),
            pltpu.VMEM((2, PATCH, PATCH), F32),
            *reduction_scratch(),
            pltpu.SemaphoreType.DMA((copies,)),
            pltpu.SemaphoreType.DMA((copies,)),
        ],
        compiler_params=pltpu.CompilerParams(
            vmem_limit_bytes=48 * 2**20, collective_id=2, has_side_effects=True
        ),
        cost_estimate=pl.CostEstimate(
            flops=10**9, bytes_accessed=14 * 10**6, transcendentals=0
        ),
    )(sums, extended, totals, probe)


def shards(object_field, probe, moduli, positions, counts):
    row = lax.axis_index("ty")
    col = lax.axis_index("tx")
    anchor = jnp.stack([row * TILE, col * TILE])
    offsets = positions - anchor[None, :]
    count = lax.dynamic_slice(counts, (row * lax.axis_size("tx") + col,), (1,))
    table = jnp.asarray(dft_tables())
    extended, ordered = extend(object_field, moduli, jnp.asarray(order_table()))
    sums, totals = run_slots(count, offsets, extended, probe, ordered, table)
    extended, probe = exchange(sums, extended, totals, probe)
    sums, totals = run_slots(count, offsets, extended, probe, ordered, table)
    return fold(sums, extended, totals, probe)


def solution(mesh):
    return jax.shard_map(
        shards,
        mesh=mesh,
        in_specs=(
            P(None, "ty", "tx"),
            P(),
            P(("ty", "tx"), None, None),
            P(("ty", "tx"), None),
            P(),
        ),
        out_specs=(P(None, "ty", "tx"), P()),
        check_vma=False,
    )
```

time: 1500 us -> 228 us (0.15)
  waiting for transfers between devices: 831 us -> 0 us
  starting transfers between devices: 343 us -> 0 us
  Pallas kernels: 0 us -> 211 us
  matrix products: 155 us -> 0 us
  local copies, waits for them, and re-layouts: 67 us -> 11.3 us
  other arithmetic: 47.3 us -> 0.67 us
  loops' own time: 29.4 us -> 0 us
  between operations: 16 us -> 0.69 us
    ppermute x8 -> x0, waiting for transfers between devices: 485 us -> none  [shifted(): return lax.ppermute(block, axis, route)]
    psum x2 -> x0, waiting for transfers between devices: 346 us -> none  [shards(): lax.psum((probe_numer, probe_denom), ('ty', 'tx'))]
    ppermute x8 -> x0, starting transfers between devices: 343 us -> none  [shifted(): return lax.ppermute(block, axis, route)]
    pallas_call x0 -> x5, Pallas kernels: none -> 211 us  [the longest x1 87.6 us: exchange(): pl.pallas_call(exchange_kernel, out_shape=(jax.ShapeDtypeStruct((2, EXT,...]
    dot_general x96 -> x0, matrix products: 155 us -> none  [product(): jnp.dot(left_matrix, right_matrix, precision=lax.Precision.HIGHEST, prefe...]
    dynamic_update_slice x6 -> x0, local copies, waits for them, and re-layouts: 40.5 us -> none  [visit_slot(): lax.dynamic_update_slice(object_sums, current + update, corner_at)]
    another operation x2 -> x0, loops' own time: 29.4 us -> none  [shards(): lax.fori_loop(0, own_count, visit_slot, start_totals)]
    add x18 -> x0, other arithmetic: 26.8 us -> none  [the longest x6 11.5 us: visit_slot(): current + update]
  transfers between devices with their start and end apart: 10 -> 0, of which waited for: 8 -> 0; matrix products, arithmetic and copies ran while one was open for 1% -> 0% of each run, Pallas kernels for 0% -> 0%
where the time goes in v1:
time: 228 us; the launch traced here: 224 us
  Pallas kernels  211 us (93%)
  local copies, waits for them, and re-layouts  11.3 us (5%)
    pallas_call x1, Pallas kernels, exchange(): pl.pallas_call(exchange_kernel, out_shape=(jax.ShapeDtypeStruct((2, EXT,...  87.6 us
    pallas_call x1, Pallas kernels, fold(): pl.pallas_call(fold_kernel, out_shape=(jax.ShapeDtypeStruct((2, TILE, TIL...  73.4 us
    pallas_call x1, Pallas kernels, extend(): pl.pallas_call(extend_kernel, out_shape=(jax.ShapeDtypeStruct((2, EXT, EX...  31.8 us
    pallas_call x2, Pallas kernels, run_slots(): pl.pallas_call(slots_kernel, out_shape=(jax.ShapeDtypeStruct((2, EXT, EXT...  18.4 us
    unnamed x19, local copies, waits for them, and re-layouts  10.1 us

profile of v1, /device:TPU:1, one launch (start us, length us, event | category | flops | bytes accessed | tf_op | source)
XLA Modules:
  0.0 223.9 jit_solution(703185320140942596)
XLA Ops:
  0.6 0.1 pad_add_fusion
  0.7 1.2 dynamic_slice.3.count
  1.9 0.8 copy.9
  2.7 0.6 broadcast_subtract_fusion.offsets
  3.3 0.0 copy-start
  3.3 1.6 copy-done
  4.9 0.0 copy-start.6
  4.9 0.9 copy-done.6
  5.8 31.8 %shard_map.86 = (f32[2,768,768]{2,1,0:T(8,128)}, f32[12,256,256]{2,1,0:T(8,128)S(1)}) custom-call(f32[2,512,512]{2,1,0:T(8,128)S(1)} %copy-done, f32[12,256,256]{2,1,0:T(8,128)} %moduli.1, bf16[2,256,256]{2,1,0:T(8,128)(2,1)S(1)} %copy-done.6), custom_call_target="tpu_custom_call" | custom-call | flops 1000000000 | bytes 14000000 | tf_op jit(solution)/shard_map/pallas_call | solution.py:305
  37.7 0.0 copy-start.7
  37.7 1.6 copy-done.7
  39.3 0.0 copy-start.3
  39.3 9.2 %shard_map.87 = (f32[2,768,768]{2,1,0:T(8,128)}, f32[3,256,256]{2,1,0:T(8,128)}) custom-call(s32[1]{0:T(128)} %dynamic_slice.3.count, s32[12,2]{1,0:T(8,128)} %broadcast_subtract_fusion.offsets, f32[2,768,768]{2,1,0:T(8,128)} %get-tuple-element.10.extended, f32[2,256,256]{2,1,0:T(8,128)} %probe.3, f32[12,256,256]{2,1,0:T(8,128)} %copy-done.7, ...), custom_call_target="tpu_custom_call" | custom-call | flops 6000000000 | bytes 14000000 | tf_op jit(solution)/shard_map/pallas_call | solution.py:198
  48.5 0.0 copy-done.3
  48.5 0.0 copy-start.2
  48.5 1.1 copy-done.2
  49.6 87.6 %shard_map.88 = (f32[2,768,768]{2,1,0:T(8,128)}, f32[2,256,256]{2,1,0:T(8,128)S(1)}) custom-call(f32[2,768,768]{2,1,0:T(8,128)} %get-tuple-element.12.sums, f32[2,768,768]{2,1,0:T(8,128)} %get-tuple-element.10.extended, f32[3,256,256]{2,1,0:T(8,128)S(1)} %copy-done.2, f32[2,256,256]{2,1,0:T(8,128)S(1)} %copy-done.3), custom_call_target="tpu_custom_call" | custom-call | flops 1000000000 | bytes 14000000 | tf_op jit(solution)/shard_map/pallas_call | solution.py:508
  137.2 0.0 copy-start.4
  137.2 0.8 copy-done.4
  138.0 0.0 copy-start.5
  138.0 9.2 %shard_map.89 = (f32[2,768,768]{2,1,0:T(8,128)}, f32[3,256,256]{2,1,0:T(8,128)}) custom-call(s32[1]{0:T(128)} %dynamic_slice.3.count, s32[12,2]{1,0:T(8,128)} %broadcast_subtract_fusion.offsets, f32[2,768,768]{2,1,0:T(8,128)} %get-tuple-element.14.extended, f32[2,256,256]{2,1,0:T(8,128)} %copy-done.4, f32[12,256,256]{2,1,0:T(8,128)} %copy-done.7, ...), custom_call_target="tpu_custom_call" | custom-call | flops 6000000000 | bytes 14000000 | tf_op jit(solution)/shard_map/pallas_call | solution.py:198
  147.2 0.0 copy-done.5
  147.2 0.0 copy-start.1
  147.2 1.1 copy-done.1
  148.3 73.4 %shard_map.90 = (f32[2,512,512]{2,1,0:T(8,128)S(1)}, f32[2,256,256]{2,1,0:T(8,128)S(1)}) custom-call(f32[2,768,768]{2,1,0:T(8,128)} %get-tuple-element.16.sums, f32[2,768,768]{2,1,0:T(8,128)} %get-tuple-element.14.extended, f32[3,256,256]{2,1,0:T(8,128)S(1)} %copy-done.1, f32[2,256,256]{2,1,0:T(8,128)S(1)} %copy-done.5), custom_call_target="tpu_custom_call" | custom-call | flops 1000000000 | bytes 14000000 | tf_op jit(solution)/shard_map/pallas_call | solution.py:587
  221.8 1.3 copy.12
  223.1 0.8 copy.13
Async XLA Ops:
  3.3 1.6 copy-start
  4.9 0.9 copy-start.6
  37.7 1.6 copy-start.7
  39.3 9.2 %copy-start.3 = (f32[2,256,256]{2,1,0:T(8,128)S(1)}, f32[2,256,256]{2,1,0:T(8,128)}, u32[]{:S(2)}) copy-start(f32[2,256,256]{2,1,0:T(8,128)} %probe.3) | copy-start | bytes 1572868
  48.5 1.1 copy-start.2
  137.2 0.8 copy-start.4
  138.0 9.2 %copy-start.5 = (f32[2,256,256]{2,1,0:T(8,128)S(1)}, f32[2,256,256]{2,1,0:T(8,128)}, u32[]{:S(2)}) copy-start(f32[2,256,256]{2,1,0:T(8,128)} %copy-done.4) | copy-start | bytes 1572868
  147.2 1.1 copy-start.1

commit v2 on v1

v2 whole, which is shorter than its diff:
```python
import math

import jax
import jax.numpy as jnp
from jax import lax
from jax.experimental import pallas as pl
from jax.experimental.pallas import tpu as pltpu
from jax.sharding import PartitionSpec as P

F32 = jnp.float32
BF16 = jnp.bfloat16
MESH = pl.DeviceIdType.MESH

PATCH = 256
HALF = 128
TILE = 512
EXT = 768
CAP = 12
CHUNKS = 4
CHUNK = PATCH // CHUNKS
tiny_value = 1e-06
floor_sq = 0.0625

Z0 = slice(0, 256)
Z1 = slice(256, 512)
Z2 = slice(512, 768)


def write_tables(table):
    first = lax.broadcasted_iota(jnp.int32, (HALF, HALF), 0)
    second = lax.broadcasted_iota(jnp.int32, (HALF, HALF), 1)
    for odd in range(2):
        forms = ((first * (2 * second + odd), 1.0), (second * (2 * first + odd), -1.0))
        for k, (step, sign) in enumerate(forms):
            angle = (step % PATCH).astype(F32) * (2.0 * math.pi / PATCH)
            real = jnp.cos(angle) / 16.0
            imag = jnp.sin(angle) * (-sign / 16.0)
            form = jnp.concatenate(
                [jnp.concatenate([real, imag], 1), jnp.concatenate([-imag, real], 1)], 0
            )
            at = 4 * odd + 2 * k
            table[at], table[at + 1] = split(form)


def dot(left, right):
    return jnp.dot(left, right, preferred_element_type=F32)


def split(value):
    high = value.astype(BF16)
    return high, (value - high.astype(F32)).astype(BF16)


def thirds(value):
    high = value.astype(BF16)
    rest = value - high.astype(F32)
    middle = rest.astype(BF16)
    return high, middle, (rest - middle.astype(F32)).astype(BF16)


def right_product(value, table, at):
    high, low = split(value)
    both = dot(jnp.concatenate([high, low], 0), table[at])
    return both[:PATCH] + (both[PATCH:] + dot(high, table[at + 1]))


def left_product(table, at, value):
    high, low = split(value)
    both = dot(jnp.concatenate([table[at], table[at + 1]], 0), high)
    return both[:PATCH] + (both[PATCH:] + dot(table[at], low))


def window(row, col):
    sub_shift = row % 8
    lane_shift = col % 128
    row_at = pl.multiple_of(row - sub_shift, 8)
    col_at = pl.multiple_of(col - lane_shift, 128)
    sub = lax.broadcasted_iota(jnp.int32, (33, 8, 128), 1)
    lane = lax.broadcasted_iota(jnp.int32, (33, 8, 128), 2)
    return row_at, col_at, sub_shift, lane_shift, sub, lane


def gather(ref, plane, row, col):
    row_at, col_at, sub_shift, lane_shift, sub, lane = window(row, col)
    cols = []
    for k in range(3):
        block = ref[plane, pl.ds(row_at, 264), pl.ds(col_at + 128 * k, 128)]
        cols.append(pltpu.roll(block.reshape(33, 8, 128), (128 - lane_shift) % 128, 2))
    parts = []
    for k in range(2):
        block = jnp.where(lane < 128 - lane_shift, cols[k], cols[k + 1])
        block = pltpu.roll(block, (8 - sub_shift) % 8, 1)
        block = jnp.where(sub[:32] < 8 - sub_shift, block[:32], block[1:])
        parts.append(block.reshape(PATCH, 128))
    return jnp.concatenate(parts, 1)


def scatter_add(ref, plane, row, col, update):
    row_at, col_at, sub_shift, lane_shift, sub, lane = window(row, col)
    zeros = jnp.zeros((1, 8, 128), F32)
    parts = []
    for k in range(2):
        block = pltpu.roll(update[:, 128 * k : 128 * k + 128].reshape(32, 8, 128), sub_shift, 1)
        block = jnp.where(
            sub >= sub_shift,
            jnp.concatenate([block, zeros], 0),
            jnp.concatenate([zeros, block], 0),
        )
        parts.append(pltpu.roll(block, lane_shift, 2))
    right = lane >= lane_shift
    cols = [
        jnp.where(right, parts[0], 0.0),
        jnp.where(right, parts[1], parts[0]),
        jnp.where(right, 0.0, parts[1]),
    ]
    for k in range(3):
        place = (plane, pl.ds(row_at, 264), pl.ds(col_at + 128 * k, 128))
        ref[place] += cols[k].reshape(264, 128)


def scaled(wave, modulus):
    real = wave[:HALF]
    imag = wave[HALF:]
    scale = modulus * lax.rsqrt(real * real + imag * imag + floor_sq) - 1.0
    return jnp.concatenate([real * scale, imag * scale], 0)


def visit(slot, corner, extended, probe, weighted, moduli, table, sums, totals):
    row, col = corner(slot)
    patch_real = gather(extended, 0, row, col)
    patch_imag = gather(extended, 1, row, col)
    totals[2] += patch_real * patch_real + patch_imag * patch_imag
    exit_real = probe[0] * patch_real - probe[1] * patch_imag
    exit_imag = probe[0] * patch_imag + probe[1] * patch_real
    even = jnp.concatenate(
        [exit_real[:, :HALF] + exit_real[:, HALF:], exit_imag[:, :HALF] + exit_imag[:, HALF:]], 1
    )
    odd = jnp.concatenate(
        [exit_real[:, :HALF] - exit_real[:, HALF:], exit_imag[:, :HALF] - exit_imag[:, HALF:]], 1
    )
    yield
    even = right_product(even, table, 0)
    odd = right_product(odd, table, 4)
    yield
    real = jnp.concatenate([even[:, :HALF], odd[:, :HALF]], 1)
    imag = jnp.concatenate([even[:, HALF:], odd[:, HALF:]], 1)
    even = jnp.concatenate([real[:HALF] + real[HALF:], imag[:HALF] + imag[HALF:]], 0)
    odd = jnp.concatenate([real[:HALF] - real[HALF:], imag[:HALF] - imag[HALF:]], 0)
    yield
    even = left_product(table, 2, even)
    odd = left_product(table, 6, odd)
    yield
    even = scaled(even, moduli[slot, :HALF])
    odd = scaled(odd, moduli[slot, HALF:])
    yield
    even = left_product(table, 0, even)
    odd = left_product(table, 4, odd)
    yield
    real = jnp.concatenate([even[:HALF] + odd[:HALF], even[:HALF] - odd[:HALF]], 0)
    imag = jnp.concatenate([even[HALF:] + odd[HALF:], even[HALF:] - odd[HALF:]], 0)
    even = jnp.concatenate([real[:, :HALF], imag[:, :HALF]], 1)
    odd = jnp.concatenate([real[:, HALF:], imag[:, HALF:]], 1)
    yield
    even = right_product(even, table, 2)
    odd = right_product(odd, table, 6)
    yield
    delta_real = jnp.concatenate(
        [even[:, :HALF] + odd[:, :HALF], even[:, :HALF] - odd[:, :HALF]], 1
    )
    delta_imag = jnp.concatenate(
        [even[:, HALF:] + odd[:, HALF:], even[:, HALF:] - odd[:, HALF:]], 1
    )
    totals[0] += patch_real * delta_real + patch_imag * delta_imag
    totals[1] += patch_real * delta_imag - patch_imag * delta_real
    yield
    scatter_add(sums, 0, row, col, weighted[0] * delta_real + weighted[1] * delta_imag)
    scatter_add(sums, 1, row, col, weighted[0] * delta_imag - weighted[1] * delta_real)


def visit_together(slots, *refs):
    turns = [visit(slot, *refs) for slot in slots]
    while turns:
        turns = [turn for turn in turns if next(turn, "end") != "end"]


def slots_kernel(
    counts, positions, extended, probe, moduli, table, sums, totals, weighted
):
    ty = lax.axis_index("ty")
    tx = lax.axis_index("tx")
    count = counts[ty * lax.axis_size("tx") + tx]
    peak = jnp.max(probe[0] * probe[0] + probe[1] * probe[1])
    weighted[...] = probe[...] * (1.0 / (peak + tiny_value))
    sums[...] = jnp.zeros_like(sums)
    totals[...] = jnp.zeros_like(totals)

    def corner(slot):
        return positions[0, slot] - ty * TILE, positions[1, slot] - tx * TILE

    refs = (corner, extended, probe, weighted, moduli, table, sums, totals)

    def two(pair, carry):
        visit_together([2 * pair, 2 * pair + 1], *refs)
        return carry

    def one(slot, carry):
        visit_together([slot], *refs)
        return carry

    lax.fori_loop(0, count // 2, two, 0)
    lax.fori_loop(2 * (count // 2), count, one, 0)


VMEM = pl.BlockSpec(memory_space=pltpu.VMEM)
SMEM = pl.BlockSpec(memory_space=pltpu.SMEM)
HBM = pl.BlockSpec(memory_space=pltpu.HBM)


def run_slots(counts, positions, extended, probe, moduli, table):
    return pl.pallas_call(
        slots_kernel,
        out_shape=(
            jax.ShapeDtypeStruct((2, EXT, EXT), F32),
            jax.ShapeDtypeStruct((3, PATCH, PATCH), F32),
        ),
        in_specs=[SMEM, SMEM, VMEM, VMEM, VMEM, VMEM],
        out_specs=(VMEM, VMEM),
        scratch_shapes=[
            pltpu.VMEM((2, PATCH, PATCH), F32),
        ],
        compiler_params=pltpu.CompilerParams(vmem_limit_bytes=24 * 2**20),
        cost_estimate=pl.CostEstimate(
            flops=6 * 10**9, bytes_accessed=14 * 10**6, transcendentals=0
        ),
    )(counts, positions, extended, probe, moduli, table)


class Place:
    def __init__(self):
        ty = lax.axis_index("ty")
        tx = lax.axis_index("tx")
        self.ty, self.tx = ty, tx
        self.y, self.x = ty // 4, ty % 4
        self.z, self.core = tx // 2, tx % 2
        self.up = ((ty + 15) % 16, tx)
        self.down = ((ty + 1) % 16, tx)
        self.left = (ty, (tx + 7) % 8)
        self.right = (ty, (tx + 1) % 8)
        self.other = (ty, self.z * 2 + 1 - self.core)

    def along_y(self, step):
        return (((self.y + step) % 4) * 4 + self.x, self.tx)

    def along_x(self, step):
        return (self.y * 4 + (self.x + step) % 4, self.tx)

    def along_z(self, step):
        return (self.ty, ((self.z + step) % 4) * 2 + self.core)


def greet(devices):
    barrier = pltpu.get_barrier_semaphore()
    for device in devices:
        pl.semaphore_signal(barrier, inc=1, device_id=device, device_id_type=MESH)
    pl.semaphore_wait(barrier, len(devices))


class Copies:
    def __init__(self, send, receive):
        self.send, self.receive, self.used = send, receive, 0

    def start(self, source, target, device):
        copy = pltpu.make_async_remote_copy(
            src_ref=source,
            dst_ref=target,
            send_sem=self.send.at[self.used],
            recv_sem=self.receive.at[self.used],
            device_id=device,
            device_id_type=MESH,
        )
        self.used += 1
        copy.start()
        return copy


def rows_of(zone, chunk):
    return slice(zone.start + chunk * CHUNK, zone.start + (chunk + 1) * CHUNK)


def extend_kernel(tile, moduli_far, extended, ordered, table, moduli, send, receive, arrived):
    here = Place()
    copies = Copies(send, receive)
    moduli_copy = pltpu.make_async_copy(moduli_far, moduli, arrived.at[0])
    moduli_copy.start()
    tile_copy = pltpu.make_async_copy(tile, extended.at[:, 0:TILE, 0:TILE], arrived.at[1])
    tile_copy.start()
    greet([here.up, here.down, here.left, here.right])
    above = []
    for chunk in range(CHUNKS):
        above.append(
            copies.start(
                tile.at[:, rows_of(Z0, chunk), Z0], extended.at[:, rows_of(Z2, chunk), Z0], here.up
            )
        )
    beside = [copies.start(tile.at[:, :, Z0], extended.at[:, 0:TILE, Z2], here.left)]
    beside.append(copies.start(tile.at[:, Z0, Z1], extended.at[:, Z2, Z1], here.up))

    first = lax.broadcasted_iota(jnp.int32, (PATCH, PATCH), 0)
    second = lax.broadcasted_iota(jnp.int32, (PATCH, PATCH), 1)
    rows_order = (second == 2 * (first % HALF) + first // HALF).astype(F32).astype(BF16)
    cols_order = (first == 2 * (second % HALF) + second // HALF).astype(F32).astype(BF16)

    def reorder(slot, carry):
        block = moduli[slot]
        block = sum(dot(rows_order, part) for part in thirds(block))
        ordered[slot] = sum(dot(part, cols_order) for part in thirds(block))
        return carry

    write_tables(table)
    moduli_copy.wait()
    lax.fori_loop(0, CAP, reorder, 0)
    for chunk in range(CHUNKS):
        above[chunk].wait_recv()
        beside.append(
            copies.start(
                extended.at[:, rows_of(Z2, chunk), Z0],
                extended.at[:, rows_of(Z2, chunk), Z2],
                here.left,
            )
        )
    tile_copy.wait()
    for copy in above:
        copy.wait_send()
    for copy in beside:
        copy.wait()


def extend(tile, moduli):
    copies = 2 * CHUNKS + 2
    return pl.pallas_call(
        extend_kernel,
        out_shape=(
            jax.ShapeDtypeStruct((2, EXT, EXT), F32),
            jax.ShapeDtypeStruct((CAP, PATCH, PATCH), F32),
            jax.ShapeDtypeStruct((8, PATCH, PATCH), BF16),
        ),
        in_specs=[HBM, HBM],
        out_specs=(VMEM, VMEM, VMEM),
        scratch_shapes=[
            pltpu.VMEM((CAP, PATCH, PATCH), F32),
            pltpu.SemaphoreType.DMA((copies,)),
            pltpu.SemaphoreType.DMA((copies,)),
            pltpu.SemaphoreType.DMA((2,)),
        ],
        compiler_params=pltpu.CompilerParams(
            vmem_limit_bytes=20 * 2**20, collective_id=0, has_side_effects=True
        ),
        cost_estimate=pl.CostEstimate(
            flops=10**9, bytes_accessed=14 * 10**6, transcendentals=0
        ),
    )(tile, moduli)


class Reduction:
    def __init__(self, here, copies, totals, probe, probe_out, landed, held):
        self.here, self.copies = here, copies
        self.totals, self.probe, self.probe_out = totals, probe, probe_out
        self.land_core, self.land_z, self.land_x, self.land_y = landed
        self.held_core, self.held_z, self.held_x = held
        self.in_flight = []
        self.sent = []

    def launch(self, source, target, device):
        self.in_flight.append(self.copies.start(source, target, device))

    def arrive(self):
        for copy in self.in_flight:
            copy.wait_recv()
        self.sent += self.in_flight
        self.in_flight = []

    def start(self):
        half = pl.ds(pl.multiple_of((1 - self.here.core) * HALF, HALF), HALF)
        self.launch(self.totals.at[:, half, :], self.land_core, self.here.other)

    def after_core(self):
        self.arrive()
        half = pl.ds(pl.multiple_of(self.here.core * HALF, HALF), HALF)
        self.held_core[...] = self.totals[:, half, :] + self.land_core[...]
        for step in (2, 1, 3):
            part = pl.ds(pl.multiple_of(((self.here.z + step) % 4) * 32, 32), 32)
            self.launch(
                self.held_core.at[:, part, :], self.land_z.at[step - 1], self.here.along_z(step)
            )

    def after_z(self):
        self.arrive()
        part = pl.ds(pl.multiple_of(self.here.z * 32, 32), 32)
        self.held_z[...] = (self.held_core[:, part, :] + self.land_z[0]) + (
            self.land_z[1] + self.land_z[2]
        )
        for step in (2, 1, 3):
            part = pl.ds(pl.multiple_of(((self.here.x + step) % 4) * 8, 8), 8)
            self.launch(
                self.held_z.at[:, part, :], self.land_x.at[step - 1], self.here.along_x(step)
            )

    def after_x(self):
        self.arrive()
        part = pl.ds(pl.multiple_of(self.here.x * 8, 8), 8)
        self.held_x[...] = (self.held_z[:, part, :] + self.land_x[0]) + (
            self.land_x[1] + self.land_x[2]
        )
        for step in (2, 1, 3):
            self.launch(self.held_x, self.land_y.at[self.here.y], self.here.along_y(step))
        self.land_y[self.here.y] = self.held_x[...]

    def share(self, rows):
        start = self.here.core * HALF
        if rows < 128:
            start = start + self.here.z * 32
        if rows < 32:
            start = start + self.here.x * 8
        return pl.ds(pl.multiple_of(start, rows), rows)

    def spread(self, rows, device):
        part = self.probe_out.at[:, self.share(rows), :]
        self.launch(part, part, device)

    def after_y(self):
        self.arrive()
        total = (self.land_y[0] + self.land_y[1]) + (self.land_y[2] + self.land_y[3])
        part = self.share(8)
        self.probe_out[:, part, :] = self.probe[:, part, :] + total[0:2] / (
            total[2:3] + tiny_value
        )
        for step in (2, 1, 3):
            self.spread(8, self.here.along_x(step))

    def gather_x(self):
        self.arrive()
        for step in (2, 1, 3):
            self.spread(32, self.here.along_z(step))

    def gather_z(self):
        self.arrive()
        self.spread(128, self.here.other)

    def finish(self):
        self.arrive()
        for copy in self.sent:
            copy.wait_send()


REDUCTION_COPIES = 1 + 3 + 3 + 3 + 3 + 3 + 1


def everyone(here):
    devices = [here.up, here.down, here.left, here.right, here.other]
    for step in range(1, 4):
        devices += [here.along_y(step), here.along_x(step), here.along_z(step)]
    return devices


def exchange_kernel(
    sums, extended, totals, probe, out, probe_out,
    from_left, from_up, from_down, from_right, top, bottom,
    land_core, land_z, land_x, land_y, held_core, held_z, held_x,
    send, receive,
):
    here = Place()
    copies = Copies(send, receive)
    reduction = Reduction(
        here, copies, totals, probe, probe_out,
        (land_core, land_z, land_x, land_y), (held_core, held_z, held_x),
    )
    greet(everyone(here))
    corners, outer, last = [], [], []

    def send_corner(chunk):
        pair = []
        for zone in (Z2, Z0):
            rows = rows_of(zone, chunk)
            pair.append(copies.start(sums.at[:, rows, Z2], from_left.at[:, rows, :], here.right))
        corners.append(pair)

    def take_corner(chunk):
        rows, low = rows_of(Z0, chunk), rows_of(Z2, chunk)
        for copy in corners[chunk]:
            copy.wait_recv()
        bottom[:, rows, :] = sums[:, low, Z0] + from_left[:, low, :]
        top[:, rows, :] = sums[:, rows, Z0] + from_left[:, rows, :]

    def send_outer(chunk):
        rows = rows_of(Z0, chunk)
        down = copies.start(bottom.at[:, rows, :], from_up.at[:, rows, Z0], here.down)
        up = copies.start(top.at[:, rows, :], from_down.at[:, rows, Z0], here.up)
        outer.append((down, up))

    def take_outer(chunk):
        rows, low = rows_of(Z0, chunk), rows_of(Z2, chunk)
        down, up = outer[chunk]
        down.wait_recv()
        out[:, rows, Z0] = extended[:, rows, Z0] + (top[:, rows, :] + from_up[:, rows, Z0])
        last.append(copies.start(out.at[:, rows, Z0], out.at[:, rows, Z2], here.left))
        up.wait_recv()
        out[:, low, Z0] = extended[:, low, Z0] + (bottom[:, rows, :] + from_down[:, rows, Z0])
        last.append(copies.start(out.at[:, low, Z0], out.at[:, low, Z2], here.left))

    reduction.start()
    send_corner(0)
    middle_down = copies.start(sums.at[:, Z2, Z1], from_up.at[:, :, Z1], here.down)
    middle_up = copies.start(sums.at[:, Z0, Z1], from_down.at[:, :, Z1], here.up)
    reduction.after_core()
    for chunk in range(1, CHUNKS):
        send_corner(chunk)
    side_left = copies.start(sums.at[:, Z1, Z0], from_right, here.left)
    side_right = copies.start(sums.at[:, Z1, Z2], from_left.at[:, Z1, :], here.right)
    out[:, Z1, Z1] = extended[:, Z1, Z1] + sums[:, Z1, Z1]
    reduction.after_z()
    take_corner(0)
    send_outer(0)
    middle_down.wait_recv()
    out[:, Z0, Z1] = extended[:, Z0, Z1] + (sums[:, Z0, Z1] + from_up[:, :, Z1])
    middle_up.wait_recv()
    out[:, Z2, Z1] = extended[:, Z2, Z1] + (sums[:, Z2, Z1] + from_down[:, :, Z1])
    reduction.after_x()
    for chunk in range(1, CHUNKS):
        take_corner(chunk)
    reduction.after_y()
    for chunk in range(1, CHUNKS):
        send_outer(chunk)
    side_left.wait_recv()
    out[:, Z1, Z2] = extended[:, Z1, Z2] + (sums[:, Z1, Z2] + from_right[...])
    take_outer(0)
    reduction.gather_x()
    side_right.wait_recv()
    out[:, Z1, Z0] = extended[:, Z1, Z0] + (sums[:, Z1, Z0] + from_left[:, Z1, :])
    take_outer(1)
    reduction.gather_z()
    for chunk in range(2, CHUNKS):
        take_outer(chunk)
    reduction.finish()
    for pair in corners + outer:
        for copy in pair:
            copy.wait_send()
    for copy in [middle_down, middle_up, side_left, side_right]:
        copy.wait_send()
    for copy in last:
        copy.wait()


def reduction_scratch():
    return [
        pltpu.VMEM((3, 128, PATCH), F32),
        pltpu.VMEM((3, 3, 32, PATCH), F32),
        pltpu.VMEM((3, 3, 8, PATCH), F32),
        pltpu.VMEM((4, 3, 8, PATCH), F32),
        pltpu.VMEM((3, 128, PATCH), F32),
        pltpu.VMEM((3, 32, PATCH), F32),
        pltpu.VMEM((3, 8, PATCH), F32),
    ]


def exchange(sums, extended, totals, probe):
    copies = REDUCTION_COPIES + 6 * CHUNKS + 4
    return pl.pallas_call(
        exchange_kernel,
        out_shape=(
            jax.ShapeDtypeStruct((2, EXT, EXT), F32),
            jax.ShapeDtypeStruct((2, PATCH, PATCH), F32),
        ),
        in_specs=[VMEM] * 4,
        out_specs=(VMEM, VMEM),
        scratch_shapes=[
            pltpu.VMEM((2, EXT, PATCH), F32),
            pltpu.VMEM((2, PATCH, TILE), F32),
            pltpu.VMEM((2, PATCH, TILE), F32),
            pltpu.VMEM((2, PATCH, PATCH), F32),
            pltpu.VMEM((2, PATCH, PATCH), F32),
            pltpu.VMEM((2, PATCH, PATCH), F32),
            *reduction_scratch(),
            pltpu.SemaphoreType.DMA((copies,)),
            pltpu.SemaphoreType.DMA((copies,)),
        ],
        compiler_params=pltpu.CompilerParams(
            vmem_limit_bytes=28 * 2**20, collective_id=1, has_side_effects=True
        ),
        cost_estimate=pl.CostEstimate(
            flops=10**9, bytes_accessed=14 * 10**6, transcendentals=0
        ),
    )(sums, extended, totals, probe)


def fold_kernel(
    sums, extended, totals, probe, out, probe_out,
    from_left, from_up, bottom,
    land_core, land_z, land_x, land_y, held_core, held_z, held_x,
    send, receive,
):
    here = Place()
    copies = Copies(send, receive)
    reduction = Reduction(
        here, copies, totals, probe, probe_out,
        (land_core, land_z, land_x, land_y), (held_core, held_z, held_x),
    )
    greet(everyone(here))
    corners, outer = [], []

    def send_corner(chunk):
        rows = rows_of(Z2, chunk)
        corners.append(copies.start(sums.at[:, rows, Z2], from_left.at[:, rows, :], here.right))

    def take_corner(chunk):
        rows, low = rows_of(Z0, chunk), rows_of(Z2, chunk)
        corners[chunk].wait_recv()
        bottom[:, rows, :] = sums[:, low, Z0] + from_left[:, low, :]

    def send_outer(chunk):
        rows = rows_of(Z0, chunk)
        outer.append(copies.start(bottom.at[:, rows, :], from_up.at[:, rows, Z0], here.down))

    reduction.start()
    send_corner(0)
    middle = copies.start(sums.at[:, Z2, Z1], from_up.at[:, :, Z1], here.down)
    reduction.after_core()
    for chunk in range(1, CHUNKS):
        send_corner(chunk)
    side = copies.start(sums.at[:, 0:TILE, Z2], from_left.at[:, 0:TILE, :], here.right)
    out[:, Z1, Z1] = extended[:, Z1, Z1] + sums[:, Z1, Z1]
    reduction.after_z()
    take_corner(0)
    send_outer(0)
    middle.wait_recv()
    out[:, Z0, Z1] = extended[:, Z0, Z1] + (sums[:, Z0, Z1] + from_up[:, :, Z1])
    reduction.after_x()
    for chunk in range(1, CHUNKS):
        take_corner(chunk)
    reduction.after_y()
    for chunk in range(1, CHUNKS):
        send_outer(chunk)
    side.wait_recv()
    out[:, Z1, Z0] = extended[:, Z1, Z0] + (sums[:, Z1, Z0] + from_left[:, Z1, :])
    reduction.gather_x()
    reduction.gather_z()
    for chunk in range(CHUNKS):
        rows = rows_of(Z0, chunk)
        outer[chunk].wait_recv()
        out[:, rows, Z0] = extended[:, rows, Z0] + (
            (sums[:, rows, Z0] + from_left[:, rows, :]) + from_up[:, rows, Z0]
        )
    reduction.finish()
    for copy in corners + outer + [middle, side]:
        copy.wait_send()


def fold(sums, extended, totals, probe):
    copies = REDUCTION_COPIES + 2 * CHUNKS + 2
    return pl.pallas_call(
        fold_kernel,
        out_shape=(
            jax.ShapeDtypeStruct((2, TILE, TILE), F32),
            jax.ShapeDtypeStruct((2, PATCH, PATCH), F32),
        ),
        in_specs=[VMEM] * 4,
        out_specs=(VMEM, VMEM),
        scratch_shapes=[
            pltpu.VMEM((2, EXT, PATCH), F32),
            pltpu.VMEM((2, PATCH, TILE), F32),
            pltpu.VMEM((2, PATCH, PATCH), F32),
            *reduction_scratch(),
            pltpu.SemaphoreType.DMA((copies,)),
            pltpu.SemaphoreType.DMA((copies,)),
        ],
        compiler_params=pltpu.CompilerParams(
            vmem_limit_bytes=22 * 2**20, collective_id=2, has_side_effects=True
        ),
        cost_estimate=pl.CostEstimate(
            flops=10**9, bytes_accessed=14 * 10**6, transcendentals=0
        ),
    )(sums, extended, totals, probe)


def shards(object_field, probe, moduli, positions, counts):
    positions = positions.T
    extended, ordered, table = extend(
        pltpu.with_memory_space_constraint(object_field, pltpu.HBM),
        pltpu.with_memory_space_constraint(moduli, pltpu.HBM),
    )
    sums, totals = run_slots(counts, positions, extended, probe, ordered, table)
    extended, probe = exchange(sums, extended, totals, probe)
    sums, totals = run_slots(counts, positions, extended, probe, ordered, table)
    return fold(sums, extended, totals, probe)


def solution(mesh):
    return jax.shard_map(
        shards,
        mesh=mesh,
        in_specs=(
            P(None, "ty", "tx"),
            P(),
            P(("ty", "tx"), None, None),
            P(("ty", "tx"), None),
            P(),
        ),
        out_specs=(P(None, "ty", "tx"), P()),
        check_vma=False,
    )
```

time: 228 us -> 141 us (0.62)
  the two profiles are of different devices: /device:TPU:1 before, /device:TPU:19 now
where the time goes in v2:
time: 141 us
  Pallas kernels  138 us (98%)
  local copies, waits for them, and re-layouts  2.13 us (2%)
    pallas_call x1, Pallas kernels, exchange(): pl.pallas_call(exchange_kernel, out_shape=(jax.ShapeDtypeStruct((2, EXT,...  51.9 us
    pallas_call x1, Pallas kernels, fold(): pl.pallas_call(fold_kernel, out_shape=(jax.ShapeDtypeStruct((2, TILE, TIL...  48.1 us
    pallas_call x1, Pallas kernels, extend(): pl.pallas_call(extend_kernel, out_shape=(jax.ShapeDtypeStruct((2, EXT, EX...  25.4 us
    pallas_call x2, Pallas kernels, run_slots(): pl.pallas_call(slots_kernel, out_shape=(jax.ShapeDtypeStruct((2, EXT, EXT...  12.7 us

profile of v2, /device:TPU:19, one launch (start us, length us, event | category | flops | bytes accessed | tf_op | source)
XLA Modules:
  0.0 141.0 jit_solution(4100982563542070627)
XLA Ops:
  0.6 0.0 copy-start.2
  0.6 0.0 copy-start
  0.7 0.0 copy-start.1
  0.7 25.4 %shard_map.68 = (f32[2,768,768]{2,1,0:T(8,128)S(1)}, f32[12,256,256]{2,1,0:T(8,128)S(1)}, bf16[8,256,256]{2,1,0:T(8,128)(2,1)S(1)}) custom-call(f32[2,512,512]{2,1,0:T(8,128)} %tile.1, f32[12,256,256]{2,1,0:T(8,128)} %moduli_far.1), custom_call_target="tpu_custom_call" | custom-call | flops 1000000000 | bytes 14000000 | tf_op jit(solution)/shard_map/pallas_call | solution.py:340
  26.1 0.0 copy-done.2
  26.1 0.0 copy-done
  26.1 0.0 copy-done.1
  26.1 6.4 %shard_map.69 = (f32[2,768,768]{2,1,0:T(8,128)S(1)}, f32[3,256,256]{2,1,0:T(8,128)S(1)}) custom-call(s32[128]{0:T(128)S(1)} %copy-done.2, s32[2,12]{1,0:T(2,128)S(1)} %bitcast.1, f32[2,768,768]{2,1,0:T(8,128)S(1)} %get-tuple-element.11.extended, f32[2,256,256]{2,1,0:T(8,128)S(1)} %copy-done, f32[12,256,256]{2,1,0:T(8,128)S(1)} %get-tuple-element.12.moduli, ...), custom_call_target="tpu_custom_call" | custom-call | flops 6000000000 | bytes 14000000 | tf_op jit(solution)/shard_map/pallas_call | solution.py:220
  32.5 51.9 %shard_map.70 = (f32[2,768,768]{2,1,0:T(8,128)S(1)}, f32[2,256,256]{2,1,0:T(8,128)S(1)}) custom-call(f32[2,768,768]{2,1,0:T(8,128)S(1)} %get-tuple-element.14.sums, f32[2,768,768]{2,1,0:T(8,128)S(1)} %get-tuple-element.11.extended, f32[3,256,256]{2,1,0:T(8,128)S(1)} %get-tuple-element.15.totals, f32[2,256,256]{2,1,0:T(8,128)S(1)} %copy-done), custom_call_target="tpu_custom_call" | custom-call | flops 1000000000 | bytes 14000000 | tf_op jit(solution)/shard_map/pallas_call | solution.py:567
  84.4 6.3 %shard_map.71 = (f32[2,768,768]{2,1,0:T(8,128)S(1)}, f32[3,256,256]{2,1,0:T(8,128)S(1)}) custom-call(s32[128]{0:T(128)S(1)} %copy-done.2, s32[2,12]{1,0:T(2,128)S(1)} %bitcast.2, f32[2,768,768]{2,1,0:T(8,128)S(1)} %get-tuple-element.16.extended, f32[2,256,256]{2,1,0:T(8,128)S(1)} %get-tuple-element.17.probe, f32[12,256,256]{2,1,0:T(8,128)S(1)} %get-tuple-element.12.moduli, ...), custom_call_target="tpu_custom_call" | custom-call | flops 6000000000 | bytes 14000000 | tf_op jit(solution)/shard_map/pallas_call | solution.py:220
  90.7 48.1 %shard_map.72 = (f32[2,512,512]{2,1,0:T(8,128)S(1)}, f32[2,256,256]{2,1,0:T(8,128)S(1)}) custom-call(f32[2,768,768]{2,1,0:T(8,128)S(1)} %get-tuple-element.18.sums, f32[2,768,768]{2,1,0:T(8,128)S(1)} %get-tuple-element.16.extended, f32[3,256,256]{2,1,0:T(8,128)S(1)} %get-tuple-element.19.totals, f32[2,256,256]{2,1,0:T(8,128)S(1)} %get-tuple-element.17.probe), custom_call_target="tpu_custom_call" | custom-call | flops 1000000000 | bytes 14000000 | tf_op jit(solution)/shard_map/pallas_call | solution.py:659
  138.9 1.3 copy.9
  140.2 0.8 copy.10
Async XLA Ops:
  0.6 25.5 %copy-start.2 = (s32[128]{0:T(128)S(1)}, s32[128]{0:T(128)}, u32[]{:S(2)}) copy-start(s32[128]{0:T(128)} %counts.3) | copy-start | bytes 1540
  0.6 25.5 %copy-start = (f32[2,256,256]{2,1,0:T(8,128)S(1)}, f32[2,256,256]{2,1,0:T(8,128)}, u32[]{:S(2)}) copy-start(f32[2,256,256]{2,1,0:T(8,128)} %probe.3) | copy-start | bytes 1572868
  0.7 25.5 %copy-start.1 = (s32[12,2]{0,1:T(2,128)S(1)}, s32[12,2]{0,1:T(2,128)}, u32[]{:S(2)}) copy-start(s32[12,2]{0,1:T(2,128)} %param.8) | copy-start | bytes 292

commit v3 on v2

--- a/solution.py
+++ b/solution.py
@@ -16,6 +16,8 @@
 TILE = 512
 EXT = 768
 CAP = 12
+NEAR = 4
+EARLY = 8
 CHUNKS = 4
 CHUNK = PATCH // CHUNKS
 tiny_value = 1e-06
@@ -71,10 +73,10 @@
 
 
 def window(row, col):
-    sub_shift = row % 8
-    lane_shift = col % 128
-    row_at = pl.multiple_of(row - sub_shift, 8)
-    col_at = pl.multiple_of(col - lane_shift, 128)
+    row_at = lax.shift_right_logical(row, 3) * 8
+    col_at = lax.shift_right_logical(col, 7) * 128
+    sub_shift = row - row_at
+    lane_shift = col - col_at
     sub = lax.broadcasted_iota(jnp.int32, (33, 8, 128), 1)
     lane = lax.broadcasted_iota(jnp.int32, (33, 8, 128), 2)
     return row_at, col_at, sub_shift, lane_shift, sub, lane
@@ -85,11 +87,11 @@
     cols = []
     for k in range(3):
         block = ref[plane, pl.ds(row_at, 264), pl.ds(col_at + 128 * k, 128)]
-        cols.append(pltpu.roll(block.reshape(33, 8, 128), (128 - lane_shift) % 128, 2))
+        cols.append(pltpu.roll(block.reshape(33, 8, 128), (128 - lane_shift) & 127, 2))
     parts = []
     for k in range(2):
         block = jnp.where(lane < 128 - lane_shift, cols[k], cols[k + 1])
-        block = pltpu.roll(block, (8 - sub_shift) % 8, 1)
+        block = pltpu.roll(block, (8 - sub_shift) & 7, 1)
         block = jnp.where(sub[:32] < 8 - sub_shift, block[:32], block[1:])
         parts.append(block.reshape(PATCH, 128))
     return jnp.concatenate(parts, 1)
@@ -125,11 +127,13 @@
     return jnp.concatenate([real * scale, imag * scale], 0)
 
 
-def visit(slot, corner, extended, probe, weighted, moduli, table, sums, totals):
-    row, col = corner(slot)
-    patch_real = gather(extended, 0, row, col)
-    patch_imag = gather(extended, 1, row, col)
-    totals[2] += patch_real * patch_real + patch_imag * patch_imag
+def visit(slot, row, col, keep, source, probe, weighted, moduli, table, totals, deliver):
+    patch_real = gather(source, 0, row, col)
+    patch_imag = gather(source, 1, row, col)
+    kept_real, kept_imag = patch_real, patch_imag
+    if keep is not None:
+        kept_real, kept_imag = patch_real * keep, patch_imag * keep
+    totals[2] += patch_real * kept_real + patch_imag * kept_imag
     exit_real = probe[0] * patch_real - probe[1] * patch_imag
     exit_imag = probe[0] * patch_imag + probe[1] * patch_real
     even = jnp.concatenate(
@@ -170,45 +174,109 @@
     delta_imag = jnp.concatenate(
         [even[:, HALF:] + odd[:, HALF:], even[:, HALF:] - odd[:, HALF:]], 1
     )
-    totals[0] += patch_real * delta_real + patch_imag * delta_imag
-    totals[1] += patch_real * delta_imag - patch_imag * delta_real
+    totals[0] += kept_real * delta_real + kept_imag * delta_imag
+    totals[1] += kept_real * delta_imag - kept_imag * delta_real
     yield
-    scatter_add(sums, 0, row, col, weighted[0] * delta_real + weighted[1] * delta_imag)
-    scatter_add(sums, 1, row, col, weighted[0] * delta_imag - weighted[1] * delta_real)
-
-
-def visit_together(slots, *refs):
-    turns = [visit(slot, *refs) for slot in slots]
+    deliver(0, weighted[0] * delta_real + weighted[1] * delta_imag)
+    deliver(1, weighted[0] * delta_imag - weighted[1] * delta_real)
+
+
+def together(turns):
     while turns:
         turns = [turn for turn in turns if next(turn, "end") != "end"]
 
 
-def slots_kernel(
-    counts, positions, extended, probe, moduli, table, sums, totals, weighted
-):
-    ty = lax.axis_index("ty")
-    tx = lax.axis_index("tx")
-    count = counts[ty * lax.axis_size("tx") + tx]
+class Slots:
+    def __init__(self, counts, positions):
+        self.positions = positions
+        self.ty = lax.axis_index("ty")
+        self.tx = lax.axis_index("tx")
+        self.count = counts[self.ty * lax.axis_size("tx") + self.tx]
+        self.place = []
+        near, far = jnp.int32(0), jnp.int32(NEAR)
+        for slot in range(CAP):
+            used = slot < self.count
+            takes_near = used & (self.row(slot) <= TILE - PATCH) & (near < NEAR)
+            takes_far = used & (self.row(slot) <= TILE - HALF) & (far < EARLY)
+            place = jnp.where(takes_near, near, jnp.where(takes_far, far, -1))
+            near = near + takes_near.astype(jnp.int32)
+            far = far + jnp.where(takes_near, 0, takes_far.astype(jnp.int32))
+            self.place.append(place)
+
+    def row(self, slot):
+        return self.positions[0, slot] - self.ty * TILE
+
+    def col(self, slot):
+        return self.positions[1, slot] - self.tx * TILE
+
+    def at(self, place):
+        found, present = jnp.int32(0), jnp.int32(0)
+        for slot in range(CAP):
+            chosen = self.place[slot] == place
+            found = jnp.where(chosen, slot, found)
+            present = jnp.where(chosen, 1, present)
+        return found, present
+
+
+def write_weighted(weighted, probe):
     peak = jnp.max(probe[0] * probe[0] + probe[1] * probe[1])
     weighted[...] = probe[...] * (1.0 / (peak + tiny_value))
+
+
+def slots_kernel(
+    first, counts, positions, extended, probe, moduli, table, updates, totals_in,
+    sums, totals, weighted, queue,
+):
+    slots = Slots(counts, positions)
+    write_weighted(weighted, probe)
     sums[...] = jnp.zeros_like(sums)
-    totals[...] = jnp.zeros_like(totals)
-
-    def corner(slot):
-        return positions[0, slot] - ty * TILE, positions[1, slot] - tx * TILE
-
-    refs = (corner, extended, probe, weighted, moduli, table, sums, totals)
+
+    def turn(slot):
+        row, col = slots.row(slot), slots.col(slot)
+
+        def deliver(plane, update):
+            scatter_add(sums, plane, row, col, update)
+
+        return visit(
+            slot, row, col, None, extended, probe, weighted, moduli, table, totals, deliver
+        )
+
+    left = jnp.int32(0)
+    if first:
+        totals[...] = totals_in[...]
+
+        def add_early(index, carry):
+            slot, present = slots.at(index)
+
+            @pl.when(present == 1)
+            def _():
+                for plane in range(2):
+                    update = updates[index, plane]
+                    scatter_add(sums, plane, slots.row(slot), slots.col(slot), update)
+
+            return carry
+
+        lax.fori_loop(0, EARLY, add_early, 0)
+        for slot in range(CAP):
+            queue[left] = slot
+            late = (slot < slots.count) & (slots.place[slot] < 0)
+            left = left + late.astype(jnp.int32)
+        pick = lambda index: queue[index]
+    else:
+        totals[...] = jnp.zeros_like(totals)
+        left = slots.count
+        pick = lambda index: index
 
     def two(pair, carry):
-        visit_together([2 * pair, 2 * pair + 1], *refs)
+        together([turn(pick(2 * pair)), turn(pick(2 * pair + 1))])
         return carry
 
-    def one(slot, carry):
-        visit_together([slot], *refs)
+    def one(index, carry):
+        together([turn(pick(index))])
         return carry
 
-    lax.fori_loop(0, count // 2, two, 0)
-    lax.fori_loop(2 * (count // 2), count, one, 0)
+    lax.fori_loop(0, left // 2, two, 0)
+    lax.fori_loop(2 * (left // 2), left, one, 0)
 
 
 VMEM = pl.BlockSpec(memory_space=pltpu.VMEM)
@@ -216,23 +284,32 @@
 HBM = pl.BlockSpec(memory_space=pltpu.HBM)
 
 
-def run_slots(counts, positions, extended, probe, moduli, table):
+def run_slots(counts, positions, extended, probe, moduli, table, updates=None, totals=None):
+    first = updates is not None
+
+    def kernel(*refs):
+        refs = list(refs)
+        if not first:
+            refs[6:6] = [None, None]
+        slots_kernel(first, *refs)
+
+    operands = [counts, positions, extended, probe, moduli, table]
+    if first:
+        operands += [updates, totals]
     return pl.pallas_call(
-        slots_kernel,
+        kernel,
         out_shape=(
             jax.ShapeDtypeStruct((2, EXT, EXT), F32),
             jax.ShapeDtypeStruct((3, PATCH, PATCH), F32),
         ),
-        in_specs=[SMEM, SMEM, VMEM, VMEM, VMEM, VMEM],
+        in_specs=[SMEM, SMEM] + [VMEM] * (len(operands) - 2),
         out_specs=(VMEM, VMEM),
-        scratch_shapes=[
-            pltpu.VMEM((2, PATCH, PATCH), F32),
-        ],
+        scratch_shapes=[pltpu.VMEM((2, PATCH, PATCH), F32), pltpu.SMEM((CAP,), jnp.int32)],
         compiler_params=pltpu.CompilerParams(vmem_limit_bytes=24 * 2**20),
         cost_estimate=pl.CostEstimate(
             flops=6 * 10**9, bytes_accessed=14 * 10**6, transcendentals=0
         ),
-    )(counts, positions, extended, probe, moduli, table)
+    )(*operands)
 
 
 class Place:
@@ -287,23 +364,32 @@
     return slice(zone.start + chunk * CHUNK, zone.start + (chunk + 1) * CHUNK)
 
 
-def extend_kernel(tile, moduli_far, extended, ordered, table, moduli, send, receive, arrived):
+def extend_kernel(
+    counts, positions, probe, tile, moduli_far,
+    extended, ordered, table, updates, totals,
+    moduli, near, weighted, send, receive, arrived,
+):
     here = Place()
     copies = Copies(send, receive)
     moduli_copy = pltpu.make_async_copy(moduli_far, moduli, arrived.at[0])
     moduli_copy.start()
     tile_copy = pltpu.make_async_copy(tile, extended.at[:, 0:TILE, 0:TILE], arrived.at[1])
     tile_copy.start()
+    near_copy = pltpu.make_async_copy(tile, near.at[:, 0:TILE, 0:TILE], arrived.at[2])
+    near_copy.start()
     greet([here.up, here.down, here.left, here.right])
-    above = []
+    above, middle = [], []
     for chunk in range(CHUNKS):
         above.append(
             copies.start(
                 tile.at[:, rows_of(Z0, chunk), Z0], extended.at[:, rows_of(Z2, chunk), Z0], here.up
             )
         )
-    beside = [copies.start(tile.at[:, :, Z0], extended.at[:, 0:TILE, Z2], here.left)]
-    beside.append(copies.start(tile.at[:, Z0, Z1], extended.at[:, Z2, Z1], here.up))
+    side = copies.start(tile.at[:, :, Z0], near.at[:, 0:TILE, Z2], here.left)
+    for half in range(2):
+        rows = slice(half * HALF, (half + 1) * HALF)
+        low = slice(TILE + half * HALF, TILE + (half + 1) * HALF)
+        middle.append(copies.start(tile.at[:, rows, Z1], extended.at[:, low, Z1], here.up))
 
     first = lax.broadcasted_iota(jnp.int32, (PATCH, PATCH), 0)
     second = lax.broadcasted_iota(jnp.int32, (PATCH, PATCH), 1)
@@ -317,48 +403,88 @@
         return carry
 
     write_tables(table)
+    write_weighted(weighted, probe)
+    totals[...] = jnp.zeros_like(totals)
+    near[:, TILE:, :] = jnp.zeros((2, HALF + 8, EXT), F32)
     moduli_copy.wait()
     lax.fori_loop(0, CAP, reorder, 0)
+    corners = []
     for chunk in range(CHUNKS):
         above[chunk].wait_recv()
-        beside.append(
+        corners.append(
             copies.start(
                 extended.at[:, rows_of(Z2, chunk), Z0],
                 extended.at[:, rows_of(Z2, chunk), Z2],
                 here.left,
             )
         )
+    near_copy.wait()
+    side.wait_recv()
+    extended[:, 0:TILE, Z2] = near[:, 0:TILE, Z2]
+
+    slots = Slots(counts, positions)
+
+    def turn(index):
+        slot, present = slots.at(index)
+        row = jnp.clip(slots.row(slot), 0, TILE - HALF)
+        col = jnp.clip(slots.col(slot), 0, TILE - 1)
+        keep = present.astype(F32)
+
+        def deliver(plane, update):
+            updates[index, plane] = update
+
+        return visit(
+            slot, row, col, keep, near, probe, weighted, ordered, table, totals, deliver
+        )
+
+    def two(pair, carry):
+        @pl.when(pair == NEAR // 2)
+        def _():
+            middle[0].wait_recv()
+            for copy in corners[: CHUNKS // 2]:
+                copy.wait_recv()
+            near[:, TILE : TILE + HALF, :] = extended[:, TILE : TILE + HALF, :]
+
+        together([turn(2 * pair), turn(2 * pair + 1)])
+        return carry
+
+    lax.fori_loop(0, EARLY // 2, two, 0)
     tile_copy.wait()
-    for copy in above:
+    middle[1].wait_recv()
+    for copy in corners[CHUNKS // 2 :]:
+        copy.wait_recv()
+    for copy in above + middle + corners + [side]:
         copy.wait_send()
-    for copy in beside:
-        copy.wait()
-
-
-def extend(tile, moduli):
-    copies = 2 * CHUNKS + 2
+
+
+def extend(counts, positions, probe, tile, moduli):
+    copies = 2 * CHUNKS + 3
     return pl.pallas_call(
         extend_kernel,
         out_shape=(
             jax.ShapeDtypeStruct((2, EXT, EXT), F32),
             jax.ShapeDtypeStruct((CAP, PATCH, PATCH), F32),
             jax.ShapeDtypeStruct((8, PATCH, PATCH), BF16),
-        ),
-        in_specs=[HBM, HBM],
-        out_specs=(VMEM, VMEM, VMEM),
+            jax.ShapeDtypeStruct((EARLY, 2, PATCH, PATCH), F32),
+            jax.ShapeDtypeStruct((3, PATCH, PATCH), F32),
+        ),
+        in_specs=[SMEM, SMEM, VMEM, HBM, HBM],
+        out_specs=(VMEM,) * 5,
         scratch_shapes=[
             pltpu.VMEM((CAP, PATCH, PATCH), F32),
+            pltpu.VMEM((2, TILE + HALF + 8, EXT), F32),
+            pltpu.VMEM((2, PATCH, PATCH), F32),
             pltpu.SemaphoreType.DMA((copies,)),
             pltpu.SemaphoreType.DMA((copies,)),
-            pltpu.SemaphoreType.DMA((2,)),
+            pltpu.SemaphoreType.DMA((3,)),
         ],
         compiler_params=pltpu.CompilerParams(
-            vmem_limit_bytes=20 * 2**20, collective_id=0, has_side_effects=True
+            vmem_limit_bytes=30 * 2**20, collective_id=0, has_side_effects=True
         ),
         cost_estimate=pl.CostEstimate(
             flops=10**9, bytes_accessed=14 * 10**6, transcendentals=0
         ),
-    )(tile, moduli)
+    )(counts, positions, probe, tile, moduli)
 
 
 class Reduction:
@@ -683,11 +809,16 @@
 
 def shards(object_field, probe, moduli, positions, counts):
     positions = positions.T
-    extended, ordered, table = extend(
+    extended, ordered, table, updates, totals = extend(
+        counts,
+        positions,
+        probe,
         pltpu.with_memory_space_constraint(object_field, pltpu.HBM),
         pltpu.with_memory_space_constraint(moduli, pltpu.HBM),
     )
-    sums, totals = run_slots(counts, positions, extended, probe, ordered, table)
+    sums, totals = run_slots(
+        counts, positions, extended, probe, ordered, table, updates, totals
+    )
     extended, probe = exchange(sums, extended, totals, probe)
     sums, totals = run_slots(counts, positions, extended, probe, ordered, table)
     return fold(sums, extended, totals, probe)

time: 141 us -> 141 us (level)
  the two profiles are of different devices: /device:TPU:19 before, /device:TPU:11 now
where the time goes in v3:
time: 141 us
  Pallas kernels  136 us (96%)
  local copies, waits for them, and re-layouts  4.5 us (3%)
    pallas_call x1, Pallas kernels, fold(): pl.pallas_call(fold_kernel, out_shape=(jax.ShapeDtypeStruct((2, TILE, TIL...  54.9 us
    pallas_call x1, Pallas kernels, exchange(): pl.pallas_call(exchange_kernel, out_shape=(jax.ShapeDtypeStruct((2, EXT,...  47.4 us
    pallas_call x1, Pallas kernels, extend(): pl.pallas_call(extend_kernel, out_shape=(jax.ShapeDtypeStruct((2, EXT, EX...  27.1 us
    pallas_call x2, Pallas kernels, run_slots(): pl.pallas_call(kernel, out_shape=(jax.ShapeDtypeStruct((2, EXT, EXT), F32...  6.4 us
    unnamed x14, local copies, waits for them, and re-layouts  4.5 us

profile of v3, /device:TPU:11, one launch (start us, length us, event | category | flops | bytes accessed | tf_op | source)
XLA Modules:
  0.0 141.1 jit_solution(4404705846044550932)
XLA Ops:
  0.6 0.0 copy-start
  0.6 1.0 copy-done
  1.7 0.0 copy-start.2
  1.7 0.7 copy-done.2
  2.4 0.0 copy-start.4
  2.4 0.7 copy-done.4
  3.0 27.1 %shard_map.68 = (f32[2,768,768]{2,1,0:T(8,128)S(1)}, f32[12,256,256]{2,1,0:T(8,128)S(1)}, bf16[8,256,256]{2,1,0:T(8,128)(2,1)S(1)}, f32[8,2,256,256]{3,2,1,0:T(8,128)S(1)}, f32[3,256,256]{2,1,0:T(8,128)S(1)}) custom-call(s32[128]{0:T(128)S(1)} %copy-done.4, s32[2,12]{1,0:T(2,128)S(1)} %bitcast.1, f32[2,256,256]{2,1,0:T(8,128)S(1)} %copy-done, ...), custom_call_target="tpu_custom_call" | custom-call | flops 1000000000 | bytes 14000000 | tf_op jit(solution)/shard_map/pallas_call | solution.py:462
  30.1 0.0 copy-start.1
  30.2 3.2 %shard_map.69 = (f32[2,768,768]{2,1,0:T(8,128)S(1)}, f32[3,256,256]{2,1,0:T(8,128)S(1)}) custom-call(s32[128]{0:T(128)S(1)} %copy-done.4, s32[2,12]{1,0:T(2,128)S(1)} %bitcast.2, f32[2,768,768]{2,1,0:T(8,128)S(1)} %get-tuple-element.13.refs_2_.extended, f32[2,256,256]{2,1,0:T(8,128)S(1)} %copy-done, f32[12,256,256]{2,1,0:T(8,128)S(1)} %get-tuple-element.14.refs_4_, ...), custom_call_target="tpu_custom_call" | custom-call | flops 6000000000 | bytes 14000000 | tf_op jit(solution)/shard_map/pallas_call | solution.py:299
  33.4 0.0 copy-done.1
  33.4 0.0 copy-start.3
  33.4 0.0 copy-start.5
  33.4 47.4 %shard_map.70 = (f32[2,768,768]{2,1,0:T(8,128)S(1)}, f32[2,256,256]{2,1,0:T(8,128)S(1)}) custom-call(f32[2,768,768]{2,1,0:T(8,128)S(1)} %get-tuple-element.18.sums, f32[2,768,768]{2,1,0:T(8,128)S(1)} %get-tuple-element.13.refs_2_.extended, f32[3,256,256]{2,1,0:T(8,128)S(1)} %get-tuple-element.19.totals, f32[2,256,256]{2,1,0:T(8,128)S(1)} %copy-done.1), custom_call_target="tpu_custom_call" | custom-call | flops 1000000000 | bytes 14000000 | tf_op jit(solution)/shard_map/pallas_call | solution.py:693
  80.8 0.0 copy-done.3
  80.8 0.0 copy-done.5
  80.8 3.2 %shard_map.71 = (f32[2,768,768]{2,1,0:T(8,128)S(1)}, f32[3,256,256]{2,1,0:T(8,128)S(1)}) custom-call(s32[128]{0:T(128)S(1)} %copy-done.5, s32[2,12]{1,0:T(2,128)S(1)} %bitcast.3, f32[2,768,768]{2,1,0:T(8,128)S(1)} %get-tuple-element.20.refs_2_.extended, f32[2,256,256]{2,1,0:T(8,128)S(1)} %get-tuple-element.21.refs_3_.probe, ...), custom_call_target="tpu_custom_call" | custom-call | flops 6000000000 | bytes 14000000 | tf_op jit(solution)/shard_map/pallas_call | solution.py:299
  84.0 54.9 %shard_map.72 = (f32[2,512,512]{2,1,0:T(8,128)S(1)}, f32[2,256,256]{2,1,0:T(8,128)S(1)}) custom-call(f32[2,768,768]{2,1,0:T(8,128)S(1)} %get-tuple-element.22.sums, f32[2,768,768]{2,1,0:T(8,128)S(1)} %get-tuple-element.20.refs_2_.extended, f32[3,256,256]{2,1,0:T(8,128)S(1)} %get-tuple-element.23.totals, f32[2,256,256]{2,1,0:T(8,128)S(1)} %get-tuple-element.21.refs_3_.probe), custom_call_target="tpu_custom_call" | custom-call | flops 1000000000 | bytes 14000000 | tf_op jit(solution)/shard_map/pallas_call | solution.py:785
  138.9 1.3 copy.9
  140.3 0.8 copy.10
Async XLA Ops:
  0.6 1.0 copy-start
  1.7 0.7 copy-start.2
  2.4 0.7 copy-start.4
  30.1 3.2 %copy-start.1 = (f32[2,256,256]{2,1,0:T(8,128)S(1)}, f32[2,256,256]{2,1,0:T(8,128)}, u32[]{:S(2)}) copy-start(f32[2,256,256]{2,1,0:T(8,128)} %probe.3) | copy-start | bytes 1572868
  33.4 47.4 %copy-start.3 = (s32[12,2]{0,1:T(2,128)S(1)}, s32[12,2]{0,1:T(2,128)}, u32[]{:S(2)}) copy-start(s32[12,2]{0,1:T(2,128)} %param.8) | copy-start | bytes 292
  33.4 47.4 %copy-start.5 = (s32[128]{0:T(128)S(1)}, s32[128]{0:T(128)}, u32[]{:S(2)}) copy-start(s32[128]{0:T(128)} %refs_0_.3) | copy-start | bytes 1540

commit v4 on v3

--- a/solution.py
+++ b/solution.py
@@ -346,7 +346,7 @@
     def __init__(self, send, receive):
         self.send, self.receive, self.used = send, receive, 0
 
-    def start(self, source, target, device):
+    def make(self, source, target, device):
         copy = pltpu.make_async_remote_copy(
             src_ref=source,
             dst_ref=target,
@@ -356,6 +356,10 @@
             device_id_type=MESH,
         )
         self.used += 1
+        return copy
+
+    def start(self, source, target, device):
+        copy = self.make(source, target, device)
         copy.start()
         return copy
 
@@ -365,9 +369,9 @@
 
 
 def extend_kernel(
-    counts, positions, probe, tile, moduli_far,
+    counts, positions, probe_far, tile, moduli_far,
     extended, ordered, table, updates, totals,
-    moduli, near, weighted, send, receive, arrived,
+    moduli, near, probe, weighted, send, receive, arrived,
 ):
     here = Place()
     copies = Copies(send, receive)
@@ -377,6 +381,8 @@
     tile_copy.start()
     near_copy = pltpu.make_async_copy(tile, near.at[:, 0:TILE, 0:TILE], arrived.at[2])
     near_copy.start()
+    probe_copy = pltpu.make_async_copy(probe_far, probe, arrived.at[3])
+    probe_copy.start()
     greet([here.up, here.down, here.left, here.right])
     above, middle = [], []
     for chunk in range(CHUNKS):
@@ -403,6 +409,7 @@
         return carry
 
     write_tables(table)
+    probe_copy.wait()
     write_weighted(weighted, probe)
     totals[...] = jnp.zeros_like(totals)
     near[:, TILE:, :] = jnp.zeros((2, HALF + 8, EXT), F32)
@@ -468,15 +475,16 @@
             jax.ShapeDtypeStruct((EARLY, 2, PATCH, PATCH), F32),
             jax.ShapeDtypeStruct((3, PATCH, PATCH), F32),
         ),
-        in_specs=[SMEM, SMEM, VMEM, HBM, HBM],
+        in_specs=[SMEM, SMEM, HBM, HBM, HBM],
         out_specs=(VMEM,) * 5,
         scratch_shapes=[
             pltpu.VMEM((CAP, PATCH, PATCH), F32),
             pltpu.VMEM((2, TILE + HALF + 8, EXT), F32),
             pltpu.VMEM((2, PATCH, PATCH), F32),
+            pltpu.VMEM((2, PATCH, PATCH), F32),
             pltpu.SemaphoreType.DMA((copies,)),
             pltpu.SemaphoreType.DMA((copies,)),
-            pltpu.SemaphoreType.DMA((3,)),
+            pltpu.SemaphoreType.DMA((4,)),
         ],
         compiler_params=pltpu.CompilerParams(
             vmem_limit_bytes=30 * 2**20, collective_id=0, has_side_effects=True
@@ -485,6 +493,10 @@
             flops=10**9, bytes_accessed=14 * 10**6, transcendentals=0
         ),
     )(counts, positions, probe, tile, moduli)
+
+
+def is_inner(x):
+    return (x == 1) | (x == 2)
 
 
 class Reduction:
@@ -525,28 +537,45 @@
         self.held_z[...] = (self.held_core[:, part, :] + self.land_z[0]) + (
             self.land_z[1] + self.land_z[2]
         )
+        self.to_inner = []
         for step in (2, 1, 3):
-            part = pl.ds(pl.multiple_of(((self.here.x + step) % 4) * 8, 8), 8)
-            self.launch(
-                self.held_z.at[:, part, :], self.land_x.at[step - 1], self.here.along_x(step)
+            target = (self.here.x + step) % 4
+            copy = self.copies.make(
+                self.held_z.at[:, self.inner_rows(0, target), :],
+                self.land_x.at[step - 1],
+                self.here.along_x(step),
             )
+            self.to_inner.append((copy, is_inner(target)))
+            pl.when(is_inner(target))(copy.start)
+
+    def inner_rows(self, start, x):
+        rows = start + (x // 2) * 16
+        return pl.ds(pl.multiple_of(rows, 16), 16)
 
     def after_x(self):
-        self.arrive()
-        part = pl.ds(pl.multiple_of(self.here.x * 8, 8), 8)
-        self.held_x[...] = (self.held_z[:, part, :] + self.land_x[0]) + (
-            self.land_x[1] + self.land_x[2]
-        )
-        for step in (2, 1, 3):
-            self.launch(self.held_x, self.land_y.at[self.here.y], self.here.along_y(step))
-        self.land_y[self.here.y] = self.held_x[...]
+        self.across = [
+            self.copies.make(
+                self.held_x, self.land_y.at[self.here.y], self.here.along_y(step)
+            )
+            for step in (2, 1, 3)
+        ]
+
+        @pl.when(is_inner(self.here.x))
+        def _():
+            for copy, _ in self.to_inner:
+                copy.wait_recv()
+            part = self.inner_rows(0, self.here.x)
+            self.held_x[...] = (self.held_z[:, part, :] + self.land_x[0]) + (
+                self.land_x[1] + self.land_x[2]
+            )
+            for copy in self.across:
+                copy.start()
+            self.land_y[self.here.y] = self.held_x[...]
 
     def share(self, rows):
         start = self.here.core * HALF
         if rows < 128:
             start = start + self.here.z * 32
-        if rows < 32:
-            start = start + self.here.x * 8
         return pl.ds(pl.multiple_of(start, rows), rows)
 
     def spread(self, rows, device):
@@ -554,17 +583,27 @@
         self.launch(part, part, device)
 
     def after_y(self):
-        self.arrive()
-        total = (self.land_y[0] + self.land_y[1]) + (self.land_y[2] + self.land_y[3])
-        part = self.share(8)
-        self.probe_out[:, part, :] = self.probe[:, part, :] + total[0:2] / (
-            total[2:3] + tiny_value
-        )
-        for step in (2, 1, 3):
-            self.spread(8, self.here.along_x(step))
+        part = self.inner_rows(self.here.core * HALF + self.here.z * 32, self.here.x)
+        updated = self.probe_out.at[:, part, :]
+        self.from_inner = [
+            self.copies.make(updated, updated, self.here.along_x(step)) for step in (2, 1, 3)
+        ]
+
+        @pl.when(is_inner(self.here.x))
+        def _():
+            for copy in self.across:
+                copy.wait_recv()
+            total = (self.land_y[0] + self.land_y[1]) + (self.land_y[2] + self.land_y[3])
+            self.probe_out[:, part, :] = self.probe[:, part, :] + total[0:2] / (
+                total[2:3] + tiny_value
+            )
+            for copy in self.from_inner:
+                copy.start()
 
     def gather_x(self):
-        self.arrive()
+        for copy, step in zip(self.from_inner, (2, 1, 3)):
+            sender = (self.here.x + 4 - step) % 4
+            pl.when(is_inner(sender))(copy.wait_recv)
         for step in (2, 1, 3):
             self.spread(32, self.here.along_z(step))
 
@@ -576,6 +615,13 @@
         self.arrive()
         for copy in self.sent:
             copy.wait_send()
+        for copy, started in self.to_inner:
+            pl.when(started)(copy.wait_send)
+
+        @pl.when(is_inner(self.here.x))
+        def _():
+            for copy in self.across + self.from_inner:
+                copy.wait_send()
 
 
 REDUCTION_COPIES = 1 + 3 + 3 + 3 + 3 + 3 + 1
@@ -601,7 +647,7 @@
         (land_core, land_z, land_x, land_y), (held_core, held_z, held_x),
     )
     greet(everyone(here))
-    corners, outer, last = [], [], []
+    corners, outer, middle, last = [], [], [], []
 
     def send_corner(chunk):
         pair = []
@@ -633,44 +679,60 @@
         out[:, low, Z0] = extended[:, low, Z0] + (bottom[:, rows, :] + from_down[:, rows, Z0])
         last.append(copies.start(out.at[:, low, Z0], out.at[:, low, Z2], here.left))
 
+    def send_middle(chunk):
+        rows, low = rows_of(Z0, chunk), rows_of(Z2, chunk)
+        down = copies.start(sums.at[:, low, Z1], from_up.at[:, rows, Z1], here.down)
+        up = copies.start(sums.at[:, rows, Z1], from_down.at[:, rows, Z1], here.up)
+        middle.append((down, up))
+
+    def take_middle(chunk):
+        rows, low = rows_of(Z0, chunk), rows_of(Z2, chunk)
+        down, up = middle[chunk]
+        down.wait_recv()
+        out[:, rows, Z1] = extended[:, rows, Z1] + (sums[:, rows, Z1] + from_up[:, rows, Z1])
+        up.wait_recv()
+        out[:, low, Z1] = extended[:, low, Z1] + (sums[:, low, Z1] + from_down[:, rows, Z1])
+
     reduction.start()
     send_corner(0)
-    middle_down = copies.start(sums.at[:, Z2, Z1], from_up.at[:, :, Z1], here.down)
-    middle_up = copies.start(sums.at[:, Z0, Z1], from_down.at[:, :, Z1], here.up)
+    for chunk in range(3):
+        send_middle(chunk)
     reduction.after_core()
     for chunk in range(1, CHUNKS):
         send_corner(chunk)
     side_left = copies.start(sums.at[:, Z1, Z0], from_right, here.left)
     side_right = copies.start(sums.at[:, Z1, Z2], from_left.at[:, Z1, :], here.right)
     out[:, Z1, Z1] = extended[:, Z1, Z1] + sums[:, Z1, Z1]
-    reduction.after_z()
     take_corner(0)
     send_outer(0)
-    middle_down.wait_recv()
-    out[:, Z0, Z1] = extended[:, Z0, Z1] + (sums[:, Z0, Z1] + from_up[:, :, Z1])
-    middle_up.wait_recv()
-    out[:, Z2, Z1] = extended[:, Z2, Z1] + (sums[:, Z2, Z1] + from_down[:, :, Z1])
+    reduction.after_z()
+    take_corner(1)
+    send_outer(1)
     reduction.after_x()
-    for chunk in range(1, CHUNKS):
-        take_corner(chunk)
+    take_outer(0)
+    take_corner(2)
     reduction.after_y()
-    for chunk in range(1, CHUNKS):
-        send_outer(chunk)
+    send_outer(2)
+    take_corner(3)
+    send_outer(3)
+    send_middle(3)
+    take_outer(1)
     side_left.wait_recv()
     out[:, Z1, Z2] = extended[:, Z1, Z2] + (sums[:, Z1, Z2] + from_right[...])
-    take_outer(0)
     reduction.gather_x()
+    for chunk in range(3):
+        take_middle(chunk)
+    take_outer(2)
     side_right.wait_recv()
     out[:, Z1, Z0] = extended[:, Z1, Z0] + (sums[:, Z1, Z0] + from_left[:, Z1, :])
-    take_outer(1)
     reduction.gather_z()
-    for chunk in range(2, CHUNKS):
-        take_outer(chunk)
+    take_outer(3)
+    take_middle(3)
     reduction.finish()
-    for pair in corners + outer:
+    for pair in corners + outer + middle:
         for copy in pair:
             copy.wait_send()
-    for copy in [middle_down, middle_up, side_left, side_right]:
+    for copy in [side_left, side_right]:
         copy.wait_send()
     for copy in last:
         copy.wait()
@@ -680,16 +742,16 @@
     return [
         pltpu.VMEM((3, 128, PATCH), F32),
         pltpu.VMEM((3, 3, 32, PATCH), F32),
-        pltpu.VMEM((3, 3, 8, PATCH), F32),
-        pltpu.VMEM((4, 3, 8, PATCH), F32),
+        pltpu.VMEM((3, 3, 16, PATCH), F32),
+        pltpu.VMEM((4, 3, 16, PATCH), F32),
         pltpu.VMEM((3, 128, PATCH), F32),
         pltpu.VMEM((3, 32, PATCH), F32),
-        pltpu.VMEM((3, 8, PATCH), F32),
+        pltpu.VMEM((3, 16, PATCH), F32),
     ]
 
 
 def exchange(sums, extended, totals, probe):
-    copies = REDUCTION_COPIES + 6 * CHUNKS + 4
+    copies = REDUCTION_COPIES + 8 * CHUNKS + 2
     return pl.pallas_call(
         exchange_kernel,
         out_shape=(
@@ -755,15 +817,16 @@
     side = copies.start(sums.at[:, 0:TILE, Z2], from_left.at[:, 0:TILE, :], here.right)
     out[:, Z1, Z1] = extended[:, Z1, Z1] + sums[:, Z1, Z1]
     reduction.after_z()
-    take_corner(0)
-    send_outer(0)
+    for chunk in range(2):
+        take_corner(chunk)
+        send_outer(chunk)
     middle.wait_recv()
     out[:, Z0, Z1] = extended[:, Z0, Z1] + (sums[:, Z0, Z1] + from_up[:, :, Z1])
     reduction.after_x()
-    for chunk in range(1, CHUNKS):
+    for chunk in range(2, CHUNKS):
         take_corner(chunk)
     reduction.after_y()
-    for chunk in range(1, CHUNKS):
+    for chunk in range(2, CHUNKS):
         send_outer(chunk)
     side.wait_recv()
     out[:, Z1, Z0] = extended[:, Z1, Z0] + (sums[:, Z1, Z0] + from_left[:, Z1, :])
@@ -807,12 +870,37 @@
     )(sums, extended, totals, probe)
 
 
+def publish_kernel(tile, probe, tile_out, probe_out, done):
+    copies = [
+        pltpu.make_async_copy(tile, tile_out, done.at[0]),
+        pltpu.make_async_copy(probe, probe_out, done.at[1]),
+    ]
+    for copy in copies:
+        copy.start()
+    for copy in copies:
+        copy.wait()
+
+
+def publish(tile, probe):
+    return pl.pallas_call(
+        publish_kernel,
+        out_shape=(
+            jax.ShapeDtypeStruct(tile.shape, tile.dtype),
+            jax.ShapeDtypeStruct(probe.shape, probe.dtype),
+        ),
+        in_specs=[VMEM, VMEM],
+        out_specs=(HBM, HBM),
+        scratch_shapes=[pltpu.SemaphoreType.DMA((2,))],
+        compiler_params=pltpu.CompilerParams(vmem_limit_bytes=8 * 2**20),
+    )(tile, probe)
+
+
 def shards(object_field, probe, moduli, positions, counts):
     positions = positions.T
     extended, ordered, table, updates, totals = extend(
         counts,
         positions,
-        probe,
+        pltpu.with_memory_space_constraint(probe, pltpu.HBM),
         pltpu.with_memory_space_constraint(object_field, pltpu.HBM),
         pltpu.with_memory_space_constraint(moduli, pltpu.HBM),
     )
@@ -821,7 +909,7 @@
     )
     extended, probe = exchange(sums, extended, totals, probe)
     sums, totals = run_slots(counts, positions, extended, probe, ordered, table)
-    return fold(sums, extended, totals, probe)
+    return publish(*fold(sums, extended, totals, probe))
 
 
 def solution(mesh):

time: 141 us -> 131 us (0.929)
  the two profiles are of different devices: /device:TPU:11 before, /device:TPU:1 now
where the time goes in v4:
time: 131 us; the launch traced here: 130 us
  Pallas kernels  128 us (98%)
  local copies, waits for them, and re-layouts  1.4 us (1%)
    pallas_call x1, Pallas kernels, exchange(): pl.pallas_call(exchange_kernel, out_shape=(jax.ShapeDtypeStruct((2, EXT,...  41.4 us
    pallas_call x1, Pallas kernels, fold(): pl.pallas_call(fold_kernel, out_shape=(jax.ShapeDtypeStruct((2, TILE, TIL...  39.7 us
    pallas_call x1, Pallas kernels, extend(): pl.pallas_call(extend_kernel, out_shape=(jax.ShapeDtypeStruct((2, EXT, EX...  31.7 us
    pallas_call x2, Pallas kernels, run_slots(): pl.pallas_call(kernel, out_shape=(jax.ShapeDtypeStruct((2, EXT, EXT), F32...  13.8 us

profile of v4, /device:TPU:1, one launch (start us, length us, event | category | flops | bytes accessed | tf_op | source)
XLA Modules:
  0.0 130.4 jit_solution(5551670898123408353)
XLA Ops:
  0.6 0.0 copy-start
  0.6 0.0 copy-start.1
  0.7 0.7 copy-done.1
  1.4 0.0 copy-start.3
  1.4 0.7 copy-done.3
  2.0 31.7 %shard_map.68 = (f32[2,768,768]{2,1,0:T(8,128)S(1)}, f32[12,256,256]{2,1,0:T(8,128)S(1)}, bf16[8,256,256]{2,1,0:T(8,128)(2,1)S(1)}, f32[8,2,256,256]{3,2,1,0:T(8,128)S(1)}, f32[3,256,256]{2,1,0:T(8,128)S(1)}) custom-call(s32[128]{0:T(128)S(1)} %copy-done.3, s32[2,12]{1,0:T(2,128)S(1)} %bitcast.1, f32[2,256,256]{2,1,0:T(8,128)} %probe.1, ...), custom_call_target="tpu_custom_call" | custom-call | flops 1000000000 | bytes 14000000 | tf_op jit(solution)/shard_map/pallas_call | solution.py:469
  33.7 0.0 copy-done
  33.7 4.7 %shard_map.69 = (f32[2,768,768]{2,1,0:T(8,128)S(1)}, f32[3,256,256]{2,1,0:T(8,128)S(1)}) custom-call(s32[128]{0:T(128)S(1)} %copy-done.3, s32[2,12]{1,0:T(2,128)S(1)} %bitcast.2, f32[2,768,768]{2,1,0:T(8,128)S(1)} %get-tuple-element.15.refs_2_.extended, f32[2,256,256]{2,1,0:T(8,128)S(1)} %copy-done, f32[12,256,256]{2,1,0:T(8,128)S(1)} %get-tuple-element.16.refs_4_, ...), custom_call_target="tpu_custom_call" | custom-call | flops 6000000000 | bytes 14000000 | tf_op jit(solution)/shard_map/pallas_call | solution.py:299
  38.5 0.0 copy-start.2
  38.5 0.0 copy-start.4
  38.5 41.4 %shard_map.70 = (f32[2,768,768]{2,1,0:T(8,128)S(1)}, f32[2,256,256]{2,1,0:T(8,128)S(1)}) custom-call(f32[2,768,768]{2,1,0:T(8,128)S(1)} %get-tuple-element.20.sums, f32[2,768,768]{2,1,0:T(8,128)S(1)} %get-tuple-element.15.refs_2_.extended, f32[3,256,256]{2,1,0:T(8,128)S(1)} %get-tuple-element.21.totals, f32[2,256,256]{2,1,0:T(8,128)S(1)} %copy-done), custom_call_target="tpu_custom_call" | custom-call | flops 1000000000 | bytes 14000000 | tf_op jit(solution)/shard_map/pallas_call | solution.py:755
  79.9 0.0 copy-done.2
  79.9 0.0 copy-done.4
  79.9 9.1 %shard_map.71 = (f32[2,768,768]{2,1,0:T(8,128)S(1)}, f32[3,256,256]{2,1,0:T(8,128)S(1)}) custom-call(s32[128]{0:T(128)S(1)} %copy-done.4, s32[2,12]{1,0:T(2,128)S(1)} %bitcast.3, f32[2,768,768]{2,1,0:T(8,128)S(1)} %get-tuple-element.22.refs_2_.extended, f32[2,256,256]{2,1,0:T(8,128)S(1)} %get-tuple-element.23.refs_3_.probe, ...), custom_call_target="tpu_custom_call" | custom-call | flops 6000000000 | bytes 14000000 | tf_op jit(solution)/shard_map/pallas_call | solution.py:299
  89.0 39.7 %shard_map.72 = (f32[2,512,512]{2,1,0:T(8,128)S(1)}, f32[2,256,256]{2,1,0:T(8,128)S(1)}) custom-call(f32[2,768,768]{2,1,0:T(8,128)S(1)} %get-tuple-element.24.sums, f32[2,768,768]{2,1,0:T(8,128)S(1)} %get-tuple-element.22.refs_2_.extended, f32[3,256,256]{2,1,0:T(8,128)S(1)} %get-tuple-element.25.totals, f32[2,256,256]{2,1,0:T(8,128)S(1)} %get-tuple-element.23.refs_3_.probe), custom_call_target="tpu_custom_call" | custom-call | flops 1000000000 | bytes 14000000 | tf_op jit(solution)/shard_map/pallas_call | solution.py:848
  128.7 1.5 %shard_map.73 = (f32[2,512,512]{2,1,0:T(8,128)}, f32[2,256,256]{2,1,0:T(8,128)}) custom-call(f32[2,512,512]{2,1,0:T(8,128)S(1)} %get-tuple-element.26.tile, f32[2,256,256]{2,1,0:T(8,128)S(1)} %get-tuple-element.27.probe), custom_call_target="tpu_custom_call" | custom-call | tf_op jit(solution)/shard_map/pallas_call | solution.py:885
Async XLA Ops:
  0.6 33.1 %copy-start = (f32[2,256,256]{2,1,0:T(8,128)S(1)}, f32[2,256,256]{2,1,0:T(8,128)}, u32[]{:S(2)}) copy-start(f32[2,256,256]{2,1,0:T(8,128)} %probe.1) | copy-start | bytes 1572868
  0.6 0.7 copy-start.1
  1.4 0.7 copy-start.3
  38.5 41.4 %copy-start.2 = (s32[12,2]{0,1:T(2,128)S(1)}, s32[12,2]{0,1:T(2,128)}, u32[]{:S(2)}) copy-start(s32[12,2]{0,1:T(2,128)} %param.8) | copy-start | bytes 292
  38.5 41.4 %copy-start.4 = (s32[128]{0:T(128)S(1)}, s32[128]{0:T(128)}, u32[]{:S(2)}) copy-start(s32[128]{0:T(128)} %refs_0_.3) | copy-start | bytes 1540

commit v5 on v4

--- a/solution.py
+++ b/solution.py
@@ -13,6 +13,7 @@
 
 PATCH = 256
 HALF = 128
+QUARTER = 64
 TILE = 512
 EXT = 768
 CAP = 12
@@ -42,6 +43,15 @@
             )
             at = 4 * odd + 2 * k
             table[at], table[at + 1] = split(form)
+    for part in range(4):
+        for k, (point, wave) in enumerate(((second, first), (first, second))):
+            step = (point % QUARTER) * (4 * (wave % QUARTER) + part)
+            step = step + QUARTER * (wave // QUARTER - point // QUARTER)
+            angle = ((step + 2 * PATCH) % PATCH).astype(F32) * (2.0 * math.pi / PATCH)
+            high, low = split(jnp.cos(angle) / 16.0)
+            table[8 + 4 * k + part] = jnp.concatenate(
+                [jnp.concatenate([high, high], 1), jnp.concatenate([low, low], 1)], 0
+            )
 
 
 def dot(left, right):
@@ -66,10 +76,11 @@
     return both[:PATCH] + (both[PATCH:] + dot(high, table[at + 1]))
 
 
-def left_product(table, at, value):
-    high, low = split(value)
-    both = dot(jnp.concatenate([table[at], table[at + 1]], 0), high)
-    return both[:PATCH] + (both[PATCH:] + dot(table[at], low))
+def left_product(table, real, imag):
+    high, low = split(jnp.concatenate([real, imag], 0))
+    both = dot(table, jnp.concatenate([high, low], 0))
+    both = both[:HALF] + both[HALF:]
+    return both[:QUARTER], both[QUARTER:]
 
 
 def window(row, col):
@@ -120,11 +131,18 @@
         ref[place] += cols[k].reshape(264, 128)
 
 
-def scaled(wave, modulus):
-    real = wave[:HALF]
-    imag = wave[HALF:]
+def scaled(real, imag, modulus):
     scale = modulus * lax.rsqrt(real * real + imag * imag + floor_sq) - 1.0
-    return jnp.concatenate([real * scale, imag * scale], 0)
+    return real * scale, imag * scale
+
+
+def butterfly(real, imag):
+    return (
+        (real[0] + real[2], imag[0] + imag[2]),
+        (real[0] - real[2], imag[0] - imag[2]),
+        (real[1] + real[3], imag[1] + imag[3]),
+        (real[1] - real[3], imag[1] - imag[3]),
+    )
 
 
 def visit(slot, row, col, keep, source, probe, weighted, moduli, table, totals, deliver):
@@ -148,20 +166,23 @@
     yield
     real = jnp.concatenate([even[:, :HALF], odd[:, :HALF]], 1)
     imag = jnp.concatenate([even[:, HALF:], odd[:, HALF:]], 1)
-    even = jnp.concatenate([real[:HALF] + real[HALF:], imag[:HALF] + imag[HALF:]], 0)
-    odd = jnp.concatenate([real[:HALF] - real[HALF:], imag[:HALF] - imag[HALF:]], 0)
+    rows = [slice(QUARTER * k, QUARTER * (k + 1)) for k in range(4)]
+    (ar, ai), (br, bi), (cr, ci), (dr, di) = butterfly(
+        [real[at] for at in rows], [imag[at] for at in rows]
+    )
+    parts = [(ar + cr, ai + ci), (br + di, bi - dr), (ar - cr, ai - ci), (br - di, bi + dr)]
     yield
-    even = left_product(table, 2, even)
-    odd = left_product(table, 6, odd)
+    parts = [left_product(table[8 + k], *part) for k, part in enumerate(parts)]
     yield
-    even = scaled(even, moduli[slot, :HALF])
-    odd = scaled(odd, moduli[slot, HALF:])
+    parts = [scaled(*part, moduli[slot, rows[k]]) for k, part in enumerate(parts)]
     yield
-    even = left_product(table, 0, even)
-    odd = left_product(table, 4, odd)
+    parts = [left_product(table[12 + k], *part) for k, part in enumerate(parts)]
     yield
-    real = jnp.concatenate([even[:HALF] + odd[:HALF], even[:HALF] - odd[:HALF]], 0)
-    imag = jnp.concatenate([even[HALF:] + odd[HALF:], even[HALF:] - odd[HALF:]], 0)
+    (ar, ai), (br, bi), (cr, ci), (dr, di) = butterfly(
+        [part[0] for part in parts], [part[1] for part in parts]
+    )
+    real = jnp.concatenate([ar + cr, br - di, ar - cr, br + di], 0)
+    imag = jnp.concatenate([ai + ci, bi + dr, ai - ci, bi - dr], 0)
     even = jnp.concatenate([real[:, :HALF], imag[:, :HALF]], 1)
     odd = jnp.concatenate([real[:, HALF:], imag[:, HALF:]], 1)
     yield
@@ -399,7 +420,7 @@
 
     first = lax.broadcasted_iota(jnp.int32, (PATCH, PATCH), 0)
     second = lax.broadcasted_iota(jnp.int32, (PATCH, PATCH), 1)
-    rows_order = (second == 2 * (first % HALF) + first // HALF).astype(F32).astype(BF16)
+    rows_order = (second == 4 * (first % QUARTER) + first // QUARTER).astype(F32).astype(BF16)
     cols_order = (first == 2 * (second % HALF) + second // HALF).astype(F32).astype(BF16)
 
     def reorder(slot, carry):
@@ -471,7 +492,7 @@
         out_shape=(
             jax.ShapeDtypeStruct((2, EXT, EXT), F32),
             jax.ShapeDtypeStruct((CAP, PATCH, PATCH), F32),
-            jax.ShapeDtypeStruct((8, PATCH, PATCH), BF16),
+            jax.ShapeDtypeStruct((16, PATCH, PATCH), BF16),
             jax.ShapeDtypeStruct((EARLY, 2, PATCH, PATCH), F32),
             jax.ShapeDtypeStruct((3, PATCH, PATCH), F32),
         ),

time: 131 us -> 128 us (0.977)
  Pallas kernels: 128 us -> 126 us
    pallas_call x2, Pallas kernels: 13.8 us -> 8.05 us  [run_slots(): pl.pallas_call(kernel, out_shape=(jax.ShapeDtypeStruct((2, EXT, EXT), F32...]
    pallas_call x1, Pallas kernels: 41.4 us -> 44.6 us  [exchange(): pl.pallas_call(exchange_kernel, out_shape=(jax.ShapeDtypeStruct((2, EXT,...]
where the time goes in v5:
time: 128 us
  Pallas kernels  126 us (98%)
  local copies, waits for them, and re-layouts  1.4 us (1%)
    pallas_call x1, Pallas kernels, exchange(): pl.pallas_call(exchange_kernel, out_shape=(jax.ShapeDtypeStruct((2, EXT,...  44.6 us
    pallas_call x1, Pallas kernels, fold(): pl.pallas_call(fold_kernel, out_shape=(jax.ShapeDtypeStruct((2, TILE, TIL...  40.7 us
    pallas_call x1, Pallas kernels, extend(): pl.pallas_call(extend_kernel, out_shape=(jax.ShapeDtypeStruct((2, EXT, EX...  30.9 us
    pallas_call x2, Pallas kernels, run_slots(): pl.pallas_call(kernel, out_shape=(jax.ShapeDtypeStruct((2, EXT, EXT), F32...  8.05 us

profile of v5, /device:TPU:1, one launch (start us, length us, event | category | flops | bytes accessed | tf_op | source)
XLA Modules:
  0.0 128.0 jit_solution(18063953746943003099)
XLA Ops:
  0.6 0.0 copy-start
  0.6 0.0 copy-start.1
  0.7 0.7 copy-done.1
  1.4 0.0 copy-start.3
  1.4 0.7 copy-done.3
  2.0 30.9 %shard_map.68 = (f32[2,768,768]{2,1,0:T(8,128)S(1)}, f32[12,256,256]{2,1,0:T(8,128)S(1)}, bf16[16,256,256]{2,1,0:T(8,128)(2,1)S(1)}, f32[8,2,256,256]{3,2,1,0:T(8,128)S(1)}, f32[3,256,256]{2,1,0:T(8,128)S(1)}) custom-call(s32[128]{0:T(128)S(1)} %copy-done.3, s32[2,12]{1,0:T(2,128)S(1)} %bitcast.1, f32[2,256,256]{2,1,0:T(8,128)} %probe.1, ...), custom_call_target="tpu_custom_call" | custom-call | flops 1000000000 | bytes 14000000 | tf_op jit(solution)/shard_map/pallas_call | solution.py:490
  32.9 0.0 copy-done
  32.9 2.1 %shard_map.69 = (f32[2,768,768]{2,1,0:T(8,128)S(1)}, f32[3,256,256]{2,1,0:T(8,128)S(1)}) custom-call(s32[128]{0:T(128)S(1)} %copy-done.3, s32[2,12]{1,0:T(2,128)S(1)} %bitcast.2, f32[2,768,768]{2,1,0:T(8,128)S(1)} %get-tuple-element.15.refs_2_.extended, f32[2,256,256]{2,1,0:T(8,128)S(1)} %copy-done, f32[12,256,256]{2,1,0:T(8,128)S(1)} %get-tuple-element.16.refs_4_, ...), custom_call_target="tpu_custom_call" | custom-call | flops 6000000000 | bytes 14000000 | tf_op jit(solution)/shard_map/pallas_call | solution.py:320
  35.0 0.0 copy-start.2
  35.1 0.0 copy-start.4
  35.1 44.6 %shard_map.70 = (f32[2,768,768]{2,1,0:T(8,128)S(1)}, f32[2,256,256]{2,1,0:T(8,128)S(1)}) custom-call(f32[2,768,768]{2,1,0:T(8,128)S(1)} %get-tuple-element.20.sums, f32[2,768,768]{2,1,0:T(8,128)S(1)} %get-tuple-element.15.refs_2_.extended, f32[3,256,256]{2,1,0:T(8,128)S(1)} %get-tuple-element.21.totals, f32[2,256,256]{2,1,0:T(8,128)S(1)} %copy-done), custom_call_target="tpu_custom_call" | custom-call | flops 1000000000 | bytes 14000000 | tf_op jit(solution)/shard_map/pallas_call | solution.py:776
  79.6 0.0 copy-done.2
  79.6 0.0 copy-done.4
  79.7 5.9 %shard_map.71 = (f32[2,768,768]{2,1,0:T(8,128)S(1)}, f32[3,256,256]{2,1,0:T(8,128)S(1)}) custom-call(s32[128]{0:T(128)S(1)} %copy-done.4, s32[2,12]{1,0:T(2,128)S(1)} %bitcast.3, f32[2,768,768]{2,1,0:T(8,128)S(1)} %get-tuple-element.22.refs_2_.extended, f32[2,256,256]{2,1,0:T(8,128)S(1)} %get-tuple-element.23.refs_3_.probe, ...), custom_call_target="tpu_custom_call" | custom-call | flops 6000000000 | bytes 14000000 | tf_op jit(solution)/shard_map/pallas_call | solution.py:320
  85.6 40.7 %shard_map.72 = (f32[2,512,512]{2,1,0:T(8,128)S(1)}, f32[2,256,256]{2,1,0:T(8,128)S(1)}) custom-call(f32[2,768,768]{2,1,0:T(8,128)S(1)} %get-tuple-element.24.sums, f32[2,768,768]{2,1,0:T(8,128)S(1)} %get-tuple-element.22.refs_2_.extended, f32[3,256,256]{2,1,0:T(8,128)S(1)} %get-tuple-element.25.totals, f32[2,256,256]{2,1,0:T(8,128)S(1)} %get-tuple-element.23.refs_3_.probe), custom_call_target="tpu_custom_call" | custom-call | flops 1000000000 | bytes 14000000 | tf_op jit(solution)/shard_map/pallas_call | solution.py:869
  126.3 1.5 %shard_map.73 = (f32[2,512,512]{2,1,0:T(8,128)}, f32[2,256,256]{2,1,0:T(8,128)}) custom-call(f32[2,512,512]{2,1,0:T(8,128)S(1)} %get-tuple-element.26.tile, f32[2,256,256]{2,1,0:T(8,128)S(1)} %get-tuple-element.27.probe), custom_call_target="tpu_custom_call" | custom-call | tf_op jit(solution)/shard_map/pallas_call | solution.py:906
Async XLA Ops:
  0.6 32.3 %copy-start = (f32[2,256,256]{2,1,0:T(8,128)S(1)}, f32[2,256,256]{2,1,0:T(8,128)}, u32[]{:S(2)}) copy-start(f32[2,256,256]{2,1,0:T(8,128)} %probe.1) | copy-start | bytes 1572868
  0.6 0.7 copy-start.1
  1.4 0.7 copy-start.3
  35.0 44.6 %copy-start.2 = (s32[12,2]{0,1:T(2,128)S(1)}, s32[12,2]{0,1:T(2,128)}, u32[]{:S(2)}) copy-start(s32[12,2]{0,1:T(2,128)} %param.8) | copy-start | bytes 292
  35.1 44.6 %copy-start.4 = (s32[128]{0:T(128)S(1)}, s32[128]{0:T(128)}, u32[]{:S(2)}) copy-start(s32[128]{0:T(128)} %refs_0_.3) | copy-start | bytes 1540

commit v6 on v5

--- a/solution.py
+++ b/solution.py
@@ -657,7 +657,7 @@
 
 def exchange_kernel(
     sums, extended, totals, probe, out, probe_out,
-    from_left, from_up, from_down, from_right, top, bottom,
+    from_side, from_up, from_down, from_right, top, bottom,
     land_core, land_z, land_x, land_y, held_core, held_z, held_x,
     send, receive,
 ):
@@ -670,19 +670,24 @@
     greet(everyone(here))
     corners, outer, middle, last = [], [], [], []
 
+    def shared(chunk):
+        return (Z2, Z0, here.right, here.left) if chunk % 2 == 0 else (Z0, Z2, here.left, here.right)
+
     def send_corner(chunk):
+        given, _, owner, _ = shared(chunk)
         pair = []
         for zone in (Z2, Z0):
             rows = rows_of(zone, chunk)
-            pair.append(copies.start(sums.at[:, rows, Z2], from_left.at[:, rows, :], here.right))
+            pair.append(copies.start(sums.at[:, rows, given], from_side.at[:, rows, :], owner))
         corners.append(pair)
 
     def take_corner(chunk):
         rows, low = rows_of(Z0, chunk), rows_of(Z2, chunk)
+        _, kept, _, _ = shared(chunk)
         for copy in corners[chunk]:
             copy.wait_recv()
-        bottom[:, rows, :] = sums[:, low, Z0] + from_left[:, low, :]
-        top[:, rows, :] = sums[:, rows, Z0] + from_left[:, rows, :]
+        bottom[:, rows, :] = sums[:, low, kept] + from_side[:, low, :]
+        top[:, rows, :] = sums[:, rows, kept] + from_side[:, rows, :]
 
     def send_outer(chunk):
         rows = rows_of(Z0, chunk)
@@ -692,13 +697,14 @@
 
     def take_outer(chunk):
         rows, low = rows_of(Z0, chunk), rows_of(Z2, chunk)
+        given, kept, _, partner = shared(chunk)
         down, up = outer[chunk]
         down.wait_recv()
-        out[:, rows, Z0] = extended[:, rows, Z0] + (top[:, rows, :] + from_up[:, rows, Z0])
-        last.append(copies.start(out.at[:, rows, Z0], out.at[:, rows, Z2], here.left))
+        out[:, rows, kept] = extended[:, rows, kept] + (top[:, rows, :] + from_up[:, rows, Z0])
+        last.append(copies.start(out.at[:, rows, kept], out.at[:, rows, given], partner))
         up.wait_recv()
-        out[:, low, Z0] = extended[:, low, Z0] + (bottom[:, rows, :] + from_down[:, rows, Z0])
-        last.append(copies.start(out.at[:, low, Z0], out.at[:, low, Z2], here.left))
+        out[:, low, kept] = extended[:, low, kept] + (bottom[:, rows, :] + from_down[:, rows, Z0])
+        last.append(copies.start(out.at[:, low, kept], out.at[:, low, given], partner))
 
     def send_middle(chunk):
         rows, low = rows_of(Z0, chunk), rows_of(Z2, chunk)
@@ -716,13 +722,14 @@
 
     reduction.start()
     send_corner(0)
+    send_corner(1)
     for chunk in range(3):
         send_middle(chunk)
     reduction.after_core()
-    for chunk in range(1, CHUNKS):
+    for chunk in range(2, CHUNKS):
         send_corner(chunk)
     side_left = copies.start(sums.at[:, Z1, Z0], from_right, here.left)
-    side_right = copies.start(sums.at[:, Z1, Z2], from_left.at[:, Z1, :], here.right)
+    side_right = copies.start(sums.at[:, Z1, Z2], from_side.at[:, Z1, :], here.right)
     out[:, Z1, Z1] = extended[:, Z1, Z1] + sums[:, Z1, Z1]
     take_corner(0)
     send_outer(0)
@@ -732,9 +739,9 @@
     reduction.after_x()
     take_outer(0)
     take_corner(2)
-    reduction.after_y()
     send_outer(2)
     take_corner(3)
+    reduction.after_y()
     send_outer(3)
     send_middle(3)
     take_outer(1)
@@ -745,7 +752,7 @@
         take_middle(chunk)
     take_outer(2)
     side_right.wait_recv()
-    out[:, Z1, Z0] = extended[:, Z1, Z0] + (sums[:, Z1, Z0] + from_left[:, Z1, :])
+    out[:, Z1, Z0] = extended[:, Z1, Z0] + (sums[:, Z1, Z0] + from_side[:, Z1, :])
     reduction.gather_z()
     take_outer(3)
     take_middle(3)

time: 128 us -> 126 us (0.984)
  Pallas kernels: 126 us -> 124 us
    pallas_call x1, Pallas kernels: 44.6 us -> 40.2 us  [exchange(): pl.pallas_call(exchange_kernel, out_shape=(jax.ShapeDtypeStruct((2, EXT,...]
    pallas_call x1, Pallas kernels: 40.7 us -> 42.1 us  [fold(): pl.pallas_call(fold_kernel, out_shape=(jax.ShapeDtypeStruct((2, TILE, TIL...]
where the time goes in v6:
time: 126 us
  Pallas kernels  124 us (98%)
  local copies, waits for them, and re-layouts  1.4 us (1%)
    pallas_call x1, Pallas kernels, fold(): pl.pallas_call(fold_kernel, out_shape=(jax.ShapeDtypeStruct((2, TILE, TIL...  42.1 us
    pallas_call x1, Pallas kernels, exchange(): pl.pallas_call(exchange_kernel, out_shape=(jax.ShapeDtypeStruct((2, EXT,...  40.2 us
    pallas_call x1, Pallas kernels, extend(): pl.pallas_call(extend_kernel, out_shape=(jax.ShapeDtypeStruct((2, EXT, EX...  30.9 us
    pallas_call x2, Pallas kernels, run_slots(): pl.pallas_call(kernel, out_shape=(jax.ShapeDtypeStruct((2, EXT, EXT), F32...  9.15 us

profile of v6, /device:TPU:1, one launch (start us, length us, event | category | flops | bytes accessed | tf_op | source)
XLA Modules:
  0.0 126.1 jit_solution(3005611943921127495)
XLA Ops:
  0.6 0.0 copy-start
  0.6 0.0 copy-start.1
  0.7 0.7 copy-done.1
  1.4 0.0 copy-start.3
  1.4 0.7 copy-done.3
  2.0 30.9 %shard_map.68 = (f32[2,768,768]{2,1,0:T(8,128)S(1)}, f32[12,256,256]{2,1,0:T(8,128)S(1)}, bf16[16,256,256]{2,1,0:T(8,128)(2,1)S(1)}, f32[8,2,256,256]{3,2,1,0:T(8,128)S(1)}, f32[3,256,256]{2,1,0:T(8,128)S(1)}) custom-call(s32[128]{0:T(128)S(1)} %copy-done.3, s32[2,12]{1,0:T(2,128)S(1)} %bitcast.1, f32[2,256,256]{2,1,0:T(8,128)} %probe.1, ...), custom_call_target="tpu_custom_call" | custom-call | flops 1000000000 | bytes 14000000 | tf_op jit(solution)/shard_map/pallas_call | solution.py:490
  33.0 0.0 copy-done
  33.0 3.8 %shard_map.69 = (f32[2,768,768]{2,1,0:T(8,128)S(1)}, f32[3,256,256]{2,1,0:T(8,128)S(1)}) custom-call(s32[128]{0:T(128)S(1)} %copy-done.3, s32[2,12]{1,0:T(2,128)S(1)} %bitcast.2, f32[2,768,768]{2,1,0:T(8,128)S(1)} %get-tuple-element.15.refs_2_.extended, f32[2,256,256]{2,1,0:T(8,128)S(1)} %copy-done, f32[12,256,256]{2,1,0:T(8,128)S(1)} %get-tuple-element.16.refs_4_, ...), custom_call_target="tpu_custom_call" | custom-call | flops 6000000000 | bytes 14000000 | tf_op jit(solution)/shard_map/pallas_call | solution.py:320
  36.8 0.0 copy-start.2
  36.8 0.0 copy-start.4
  36.8 40.2 %shard_map.70 = (f32[2,768,768]{2,1,0:T(8,128)S(1)}, f32[2,256,256]{2,1,0:T(8,128)S(1)}) custom-call(f32[2,768,768]{2,1,0:T(8,128)S(1)} %get-tuple-element.20.sums, f32[2,768,768]{2,1,0:T(8,128)S(1)} %get-tuple-element.15.refs_2_.extended, f32[3,256,256]{2,1,0:T(8,128)S(1)} %get-tuple-element.21.totals, f32[2,256,256]{2,1,0:T(8,128)S(1)} %copy-done), custom_call_target="tpu_custom_call" | custom-call | flops 1000000000 | bytes 14000000 | tf_op jit(solution)/shard_map/pallas_call | solution.py:783
  77.0 0.0 copy-done.2
  77.0 0.0 copy-done.4
  77.0 5.3 %shard_map.71 = (f32[2,768,768]{2,1,0:T(8,128)S(1)}, f32[3,256,256]{2,1,0:T(8,128)S(1)}) custom-call(s32[128]{0:T(128)S(1)} %copy-done.4, s32[2,12]{1,0:T(2,128)S(1)} %bitcast.3, f32[2,768,768]{2,1,0:T(8,128)S(1)} %get-tuple-element.22.refs_2_.extended, f32[2,256,256]{2,1,0:T(8,128)S(1)} %get-tuple-element.23.refs_3_.probe, ...), custom_call_target="tpu_custom_call" | custom-call | flops 6000000000 | bytes 14000000 | tf_op jit(solution)/shard_map/pallas_call | solution.py:320
  82.4 42.1 %shard_map.72 = (f32[2,512,512]{2,1,0:T(8,128)S(1)}, f32[2,256,256]{2,1,0:T(8,128)S(1)}) custom-call(f32[2,768,768]{2,1,0:T(8,128)S(1)} %get-tuple-element.24.sums, f32[2,768,768]{2,1,0:T(8,128)S(1)} %get-tuple-element.22.refs_2_.extended, f32[3,256,256]{2,1,0:T(8,128)S(1)} %get-tuple-element.25.totals, f32[2,256,256]{2,1,0:T(8,128)S(1)} %get-tuple-element.23.refs_3_.probe), custom_call_target="tpu_custom_call" | custom-call | flops 1000000000 | bytes 14000000 | tf_op jit(solution)/shard_map/pallas_call | solution.py:876
  124.4 1.5 %shard_map.73 = (f32[2,512,512]{2,1,0:T(8,128)}, f32[2,256,256]{2,1,0:T(8,128)}) custom-call(f32[2,512,512]{2,1,0:T(8,128)S(1)} %get-tuple-element.26.tile, f32[2,256,256]{2,1,0:T(8,128)S(1)} %get-tuple-element.27.probe), custom_call_target="tpu_custom_call" | custom-call | tf_op jit(solution)/shard_map/pallas_call | solution.py:913
Async XLA Ops:
  0.6 32.3 %copy-start = (f32[2,256,256]{2,1,0:T(8,128)S(1)}, f32[2,256,256]{2,1,0:T(8,128)}, u32[]{:S(2)}) copy-start(f32[2,256,256]{2,1,0:T(8,128)} %probe.1) | copy-start | bytes 1572868
  0.6 0.7 copy-start.1
  1.4 0.7 copy-start.3
  36.8 40.2 %copy-start.2 = (s32[12,2]{0,1:T(2,128)S(1)}, s32[12,2]{0,1:T(2,128)}, u32[]{:S(2)}) copy-start(s32[12,2]{0,1:T(2,128)} %param.8) | copy-start | bytes 292
  36.8 40.2 %copy-start.4 = (s32[128]{0:T(128)S(1)}, s32[128]{0:T(128)}, u32[]{:S(2)}) copy-start(s32[128]{0:T(128)} %refs_0_.3) | copy-start | bytes 1540

commit v7 on v6

--- a/solution.py
+++ b/solution.py
@@ -521,7 +521,8 @@
 
 
 class Reduction:
-    def __init__(self, here, copies, totals, probe, probe_out, landed, held):
+    def __init__(self, here, copies, totals, probe, probe_out, landed, held, pieces):
+        self.pieces = pieces
         self.here, self.copies = here, copies
         self.totals, self.probe, self.probe_out = totals, probe, probe_out
         self.land_core, self.land_z, self.land_x, self.land_y = landed
@@ -629,8 +630,19 @@
             self.spread(32, self.here.along_z(step))
 
     def gather_z(self):
-        self.arrive()
-        self.spread(128, self.here.other)
+        if not self.pieces:
+            self.arrive()
+            self.spread(128, self.here.other)
+            return
+        arriving, self.in_flight = self.in_flight, []
+        self.spread(32, self.here.other)
+        for copy, step in zip(arriving, (2, 1, 3)):
+            copy.wait_recv()
+            z = (self.here.z + 4 - step) % 4
+            rows = pl.ds(pl.multiple_of(self.here.core * HALF + z * 32, 32), 32)
+            part = self.probe_out.at[:, rows, :]
+            self.launch(part, part, self.here.other)
+        self.sent += arriving
 
     def finish(self):
         self.arrive()
@@ -645,7 +657,7 @@
                 copy.wait_send()
 
 
-REDUCTION_COPIES = 1 + 3 + 3 + 3 + 3 + 3 + 1
+REDUCTION_COPIES = 1 + 3 + 3 + 3 + 3 + 3 + 4
 
 
 def everyone(here):
@@ -665,7 +677,7 @@
     copies = Copies(send, receive)
     reduction = Reduction(
         here, copies, totals, probe, probe_out,
-        (land_core, land_z, land_x, land_y), (held_core, held_z, held_x),
+        (land_core, land_z, land_x, land_y), (held_core, held_z, held_x), False,
     )
     greet(everyone(here))
     corners, outer, middle, last = [], [], [], []
@@ -818,7 +830,7 @@
     copies = Copies(send, receive)
     reduction = Reduction(
         here, copies, totals, probe, probe_out,
-        (land_core, land_z, land_x, land_y), (held_core, held_z, held_x),
+        (land_core, land_z, land_x, land_y), (held_core, held_z, held_x), True,
     )
     greet(everyone(here))
     corners, outer = [], []

time: 126 us -> 125 us (level)
  Pallas kernels: 124 us -> 122 us
    pallas_call x1, Pallas kernels: 42.1 us -> 40.6 us  [fold(): pl.pallas_call(fold_kernel, out_shape=(jax.ShapeDtypeStruct((2, TILE, TIL...]
where the time goes in v7:
time: 125 us; the launch traced here: 124 us
  Pallas kernels  122 us (98%)
  local copies, waits for them, and re-layouts  1.4 us (1%)
    pallas_call x1, Pallas kernels, fold(): pl.pallas_call(fold_kernel, out_shape=(jax.ShapeDtypeStruct((2, TILE, TIL...  40.6 us
    pallas_call x1, Pallas kernels, exchange(): pl.pallas_call(exchange_kernel, out_shape=(jax.ShapeDtypeStruct((2, EXT,...  39.5 us
    pallas_call x1, Pallas kernels, extend(): pl.pallas_call(extend_kernel, out_shape=(jax.ShapeDtypeStruct((2, EXT, EX...  30.9 us
    pallas_call x2, Pallas kernels, run_slots(): pl.pallas_call(kernel, out_shape=(jax.ShapeDtypeStruct((2, EXT, EXT), F32...  9.65 us

profile of v7, /device:TPU:1, one launch (start us, length us, event | category | flops | bytes accessed | tf_op | source)
XLA Modules:
  0.0 124.5 jit_solution(4882835009929810483)
XLA Ops:
  0.6 0.0 copy-start
  0.6 0.0 copy-start.1
  0.7 0.7 copy-done.1
  1.4 0.0 copy-start.3
  1.4 0.7 copy-done.3
  2.0 30.9 %shard_map.68 = (f32[2,768,768]{2,1,0:T(8,128)S(1)}, f32[12,256,256]{2,1,0:T(8,128)S(1)}, bf16[16,256,256]{2,1,0:T(8,128)(2,1)S(1)}, f32[8,2,256,256]{3,2,1,0:T(8,128)S(1)}, f32[3,256,256]{2,1,0:T(8,128)S(1)}) custom-call(s32[128]{0:T(128)S(1)} %copy-done.3, s32[2,12]{1,0:T(2,128)S(1)} %bitcast.1, f32[2,256,256]{2,1,0:T(8,128)} %probe.1, ...), custom_call_target="tpu_custom_call" | custom-call | flops 1000000000 | bytes 14000000 | tf_op jit(solution)/shard_map/pallas_call | solution.py:490
  32.9 0.0 copy-done
  32.9 3.7 %shard_map.69 = (f32[2,768,768]{2,1,0:T(8,128)S(1)}, f32[3,256,256]{2,1,0:T(8,128)S(1)}) custom-call(s32[128]{0:T(128)S(1)} %copy-done.3, s32[2,12]{1,0:T(2,128)S(1)} %bitcast.2, f32[2,768,768]{2,1,0:T(8,128)S(1)} %get-tuple-element.15.refs_2_.extended, f32[2,256,256]{2,1,0:T(8,128)S(1)} %copy-done, f32[12,256,256]{2,1,0:T(8,128)S(1)} %get-tuple-element.16.refs_4_, ...), custom_call_target="tpu_custom_call" | custom-call | flops 6000000000 | bytes 14000000 | tf_op jit(solution)/shard_map/pallas_call | solution.py:320
  36.6 0.0 copy-start.2
  36.7 0.0 copy-start.4
  36.7 39.5 %shard_map.70 = (f32[2,768,768]{2,1,0:T(8,128)S(1)}, f32[2,256,256]{2,1,0:T(8,128)S(1)}) custom-call(f32[2,768,768]{2,1,0:T(8,128)S(1)} %get-tuple-element.20.sums, f32[2,768,768]{2,1,0:T(8,128)S(1)} %get-tuple-element.15.refs_2_.extended, f32[3,256,256]{2,1,0:T(8,128)S(1)} %get-tuple-element.21.totals, f32[2,256,256]{2,1,0:T(8,128)S(1)} %copy-done), custom_call_target="tpu_custom_call" | custom-call | flops 1000000000 | bytes 14000000 | tf_op jit(solution)/shard_map/pallas_call | solution.py:795
  76.2 0.0 copy-done.2
  76.2 0.0 copy-done.4
  76.2 5.9 %shard_map.71 = (f32[2,768,768]{2,1,0:T(8,128)S(1)}, f32[3,256,256]{2,1,0:T(8,128)S(1)}) custom-call(s32[128]{0:T(128)S(1)} %copy-done.4, s32[2,12]{1,0:T(2,128)S(1)} %bitcast.3, f32[2,768,768]{2,1,0:T(8,128)S(1)} %get-tuple-element.22.refs_2_.extended, f32[2,256,256]{2,1,0:T(8,128)S(1)} %get-tuple-element.23.refs_3_.probe, ...), custom_call_target="tpu_custom_call" | custom-call | flops 6000000000 | bytes 14000000 | tf_op jit(solution)/shard_map/pallas_call | solution.py:320
  82.2 40.6 %shard_map.72 = (f32[2,512,512]{2,1,0:T(8,128)S(1)}, f32[2,256,256]{2,1,0:T(8,128)S(1)}) custom-call(f32[2,768,768]{2,1,0:T(8,128)S(1)} %get-tuple-element.24.sums, f32[2,768,768]{2,1,0:T(8,128)S(1)} %get-tuple-element.22.refs_2_.extended, f32[3,256,256]{2,1,0:T(8,128)S(1)} %get-tuple-element.25.totals, f32[2,256,256]{2,1,0:T(8,128)S(1)} %get-tuple-element.23.refs_3_.probe), custom_call_target="tpu_custom_call" | custom-call | flops 1000000000 | bytes 14000000 | tf_op jit(solution)/shard_map/pallas_call | solution.py:888
  122.8 1.5 %shard_map.73 = (f32[2,512,512]{2,1,0:T(8,128)}, f32[2,256,256]{2,1,0:T(8,128)}) custom-call(f32[2,512,512]{2,1,0:T(8,128)S(1)} %get-tuple-element.26.tile, f32[2,256,256]{2,1,0:T(8,128)S(1)} %get-tuple-element.27.probe), custom_call_target="tpu_custom_call" | custom-call | tf_op jit(solution)/shard_map/pallas_call | solution.py:925
Async XLA Ops:
  0.6 32.3 %copy-start = (f32[2,256,256]{2,1,0:T(8,128)S(1)}, f32[2,256,256]{2,1,0:T(8,128)}, u32[]{:S(2)}) copy-start(f32[2,256,256]{2,1,0:T(8,128)} %probe.1) | copy-start | bytes 1572868
  0.6 0.7 copy-start.1
  1.4 0.7 copy-start.3
  36.6 39.5 %copy-start.2 = (s32[12,2]{0,1:T(2,128)S(1)}, s32[12,2]{0,1:T(2,128)}, u32[]{:S(2)}) copy-start(s32[12,2]{0,1:T(2,128)} %param.8) | copy-start | bytes 292
  36.7 39.5 %copy-start.4 = (s32[128]{0:T(128)S(1)}, s32[128]{0:T(128)}, u32[]{:S(2)}) copy-start(s32[128]{0:T(128)} %refs_0_.3) | copy-start | bytes 1540
